TPU v7x, 32 devices: a whole 2x2x4 slice. The times are simulated.
32 devices in a mesh: seq: 16 (over z, y, x), head: 2 (over core).
Axes of the slice: x: 2, y: 2, z: 4, core: 2. Of those that a mesh axis runs over, the one named last changes fastest.
Arguments:
- q_in: bfloat16 [2048, 2048], P('seq', 'head'), may hold values from -6 to 6
- k_in: bfloat16 [2048, 2048], P('seq', 'head'), may hold values from -6 to 6
- v_in: bfloat16 [2048, 2048], P('seq', 'head'), may hold values from -8 to 8
- filters: bfloat16 [3, 128, 128], P(None, 'head'), may hold values from -1 to 1
- lengths: int32 [32], replicated, may hold values from 1 to 128, 2048 in all
- gain: bfloat16 [2048], P('head'), may hold values from 0.099609375 to 1.8984375
Outputs:
- normed: bfloat16 [2048, 2048], P('seq', 'head')
Inputs may be any that keep to these rules, and one draw needn't show every extreme that they name: lengths of the 32 documents packed in order along the sequence; they sum to 2048.
All inputs are finite; a program needn't handle non-finite values.
Results may differ from a plain program's by a relative error of at most 0.005.
The roundings to bfloat16 on the way count: a program that leaves them out, or rounds other values in their place, can miss the bound.
Values may be sent and summed in bfloat16 or wider, within the bound.
No kernel may reach another device: no remote copies, remote signals or barrier semaphores. Data moves between devices by JAX's collectives and lax.ppermute only.
A program may use at most 128 MiB of HBM per device.

v0:
```python
import math

import jax
import jax.numpy as jnp
from jax import lax
from jax.sharding import PartitionSpec as P

HDIM = 128


def passed_along(value, axis, steps):
    count = lax.axis_size(axis)
    initial, last = (max(0, -steps), min(count, count - steps))
    return lax.ppermute(value, axis, [(source, source + steps) for source in range(initial, last)])


def banded_pair(filter_rows):
    groups, tap_count = filter_rows.shape
    lag_index = (
        jnp.arange(tap_count, dtype=jnp.int32)[None, :]
        - jnp.arange(tap_count, dtype=jnp.int32)[:, None]
    )
    within = filter_rows[:, jnp.clip(lag_index, 0, tap_count - 1)]
    beyond = filter_rows[:, jnp.clip(lag_index + tap_count, 0, tap_count - 1)]
    current = jnp.where(lag_index[None] >= 0, within, jnp.zeros_like(within))
    earlier = jnp.where(lag_index[None] < 0, beyond, jnp.zeros_like(beyond))
    return jnp.concatenate([current, earlier], 2)


def gated_conv(signal, rim_rows, filter_rows):
    tok_count, channels = signal.shape
    groups, tap_count = filter_rows.shape
    joined = jnp.transpose(jnp.concatenate([rim_rows, signal], 0))
    span_len = tok_count + tap_count
    rows = joined.reshape(groups, channels // groups * (span_len // tap_count), tap_count)
    stacked = banded_pair(filter_rows)
    both = jnp.einsum("grj,gji->gri", rows, stacked, preferred_element_type=jnp.float32)
    now_part = both[:, :, :tap_count].reshape(channels, span_len)[:, tap_count:]
    prev_part = both[:, :, tap_count:].reshape(channels, span_len)[:, :tok_count]
    convolved = now_part + prev_part
    return (joined[:, tap_count:].astype(jnp.float32) * convolved).astype(jnp.bfloat16)


def doc_index(positions, doc_ends):
    return jnp.sum((doc_ends[None, :] <= positions[:, None]).astype(jnp.int32), axis=1)


def attend(q_cols, q_pos, k_cols, v_cols, k_pos, doc_ends):
    allowed = doc_index(q_pos, doc_ends)[:, None] == doc_index(k_pos, doc_ends)[None, :]
    allowed = allowed & (k_pos[None, :] <= q_pos[:, None]) & (k_pos[None, :] >= 0)
    channels, q_rows = q_cols.shape
    head_count = channels // HDIM
    factor = 1.0 / math.sqrt(HDIM)
    inner = (((0,), (0,)), ((), ()))
    outer = (((1,), (1,)), ((), ()))
    results = []
    for head in range(head_count):
        rows = slice(head * HDIM, (head + 1) * HDIM)
        q_head = q_cols[rows]
        k_head = k_cols[rows]
        v_head = v_cols[rows]
        scores = lax.dot_general(q_head, k_head, inner, preferred_element_type=jnp.float32) * factor
        scores = jnp.where(allowed, scores, -1e30)
        top_score = jnp.max(scores, axis=1, keepdims=True)
        weights = jnp.exp(scores - top_score)
        totals = jnp.sum(weights, axis=1)
        rounded = weights.astype(jnp.bfloat16)
        mixed = lax.dot_general(rounded, v_head, outer, preferred_element_type=jnp.float32)
        results.append(mixed / totals[:, None])
    return jnp.concatenate(results, 1).astype(jnp.bfloat16)


def per_device(q_in, k_in, v_in, filters, lengths, gain):
    tok_rows, channels = q_in.shape
    seq_index = lax.axis_index("seq")
    doc_ends = jnp.cumsum(lengths)
    rim_q, rim_k, rim_v = passed_along((q_in, k_in, v_in), "seq", 1)
    queries = gated_conv(q_in, rim_q, filters[0])
    keys = gated_conv(k_in, rim_k, filters[1])
    values = gated_conv(v_in, rim_v, filters[2])
    prior_k, prior_v = passed_along((keys, values), "seq", 1)
    own_pos = seq_index * tok_rows + jnp.arange(tok_rows, dtype=jnp.int32)
    prior_pos = own_pos - tok_rows
    attended = attend(
        queries,
        own_pos,
        jnp.concatenate([prior_k, keys], 1),
        jnp.concatenate([prior_v, values], 1),
        jnp.concatenate([prior_pos, own_pos], 0),
        doc_ends,
    )
    widened = attended.astype(jnp.float32)
    local_squares = jnp.sum(widened * widened, axis=1)
    total_squares = lax.psum(local_squares, "head")
    mean_square = total_squares / (channels * lax.axis_size("head"))
    normed = widened * lax.rsqrt(mean_square + 1e-06)[:, None] * gain.astype(jnp.float32)[None, :]
    return normed.astype(jnp.bfloat16)


def solution(mesh):
    placed = (
        P("seq", "head"),
        P("seq", "head"),
        P("seq", "head"),
        P(None, "head", None),
        P(),
        P("head"),
    )
    return jax.shard_map(
        per_device, mesh=mesh, in_specs=placed, out_specs=P("seq", "head"), check_vma=False
    )
```

profile of v0, /device:TPU:9, one launch (start us, length us, event | category | flops | bytes accessed | tf_op | source)
XLA Modules:
  0.0 459.5 jit_solution(5546151453648899819)
XLA Ops:
  0.0 3.1 collective-permute-start.1
  3.1 3.1 collective-permute-start
  6.2 3.1 collective-permute-start.3
  10.3 57.4 %gather_fusion = bf16[16384,64]{1,0:T(8,128)(2,1)} fusion(bf16[64,128]{0,1:T(8,128)(2,1)S(1)} %bitcast.41, s32[16384]{0:T(1024)S(1)} %fusion.92), kind=kCustom, calls=%fused_computation | custom fusion | bytes 4259840 | tf_op jit(solution)/shard_map/gather | solution.py:23
  67.7 57.4 %gather_fusion.1 = bf16[16384,64]{1,0:T(8,128)(2,1)} fusion(bf16[64,128]{0,1:T(8,128)(2,1)S(1)} %bitcast.42, s32[16384]{0:T(1024)S(1)} %fusion.94), kind=kCustom, calls=%fused_computation.1 | custom fusion | bytes 4259840 | tf_op jit(solution)/shard_map/gather | solution.py:24
  125.2 57.4 %gather_fusion.2 = bf16[16384,64]{1,0:T(8,128)(2,1)} fusion(bf16[64,128]{0,1:T(8,128)(2,1)S(1)} %bitcast.43, s32[16384]{0:T(1024)S(1)} %fusion.92), kind=kCustom, calls=%fused_computation.2 | custom fusion | bytes 4259840 | tf_op jit(solution)/shard_map/gather | solution.py:23
  182.6 57.4 %gather_fusion.3 = bf16[16384,64]{1,0:T(8,128)(2,1)} fusion(bf16[64,128]{0,1:T(8,128)(2,1)S(1)} %bitcast.44, s32[16384]{0:T(1024)S(1)} %fusion.94), kind=kCustom, calls=%fused_computation.3 | custom fusion | bytes 4259840 | tf_op jit(solution)/shard_map/gather | solution.py:24
  240.1 57.4 %gather_fusion.4 = bf16[16384,64]{1,0:T(8,128)(2,1)} fusion(bf16[64,128]{0,1:T(8,128)(2,1)S(1)} %bitcast.39, s32[16384]{0:T(1024)S(1)} %fusion.92), kind=kCustom, calls=%fused_computation.4 | custom fusion | bytes 4259840 | tf_op jit(solution)/shard_map/gather | solution.py:23
  297.5 57.4 %gather_fusion.5 = bf16[16384,64]{1,0:T(8,128)(2,1)} fusion(bf16[64,128]{0,1:T(8,128)(2,1)S(1)} %bitcast.40, s32[16384]{0:T(1024)S(1)} %fusion.94), kind=kCustom, calls=%fused_computation.5 | custom fusion | bytes 4259840 | tf_op jit(solution)/shard_map/gather | solution.py:24
  354.9 4.8 %copy.67 = bf16[128,128,64]{1,0,2:T(8,128)(2,1)S(1)} copy(bf16[128,128,64]{2,1,0:T(8,128)(2,1)} %bitcast.46) | data formatting | bytes 4194304 | tf_op jit(solution)/shard_map/gather | solution.py:23
  359.7 5.7 %copy.68 = bf16[128,128,64]{1,0,2:T(8,128)(2,1)} copy(bf16[128,128,64]{2,1,0:T(8,128)(2,1)} %bitcast.45) | data formatting | bytes 4194304 | tf_op jit(solution)/shard_map/gather | solution.py:24
  365.4 5.6 %copy.69 = bf16[128,128,64]{1,0,2:T(8,128)(2,1)} copy(bf16[128,128,64]{2,1,0:T(8,128)(2,1)} %bitcast.48) | data formatting | bytes 4194304 | tf_op jit(solution)/shard_map/gather | solution.py:23
  371.0 5.6 %copy.70 = bf16[128,128,64]{1,0,2:T(8,128)(2,1)} copy(bf16[128,128,64]{2,1,0:T(8,128)(2,1)} %bitcast.47) | data formatting | bytes 4194304 | tf_op jit(solution)/shard_map/gather | solution.py:24
  376.7 5.6 %copy.71 = bf16[128,128,64]{1,0,2:T(8,128)(2,1)} copy(bf16[128,128,64]{2,1,0:T(8,128)(2,1)} %bitcast.49) | data formatting | bytes 4194304 | tf_op jit(solution)/shard_map/gather | solution.py:23
  382.3 5.6 %copy.72 = bf16[128,128,64]{1,0,2:T(8,128)(2,1)} copy(bf16[128,128,64]{2,1,0:T(8,128)(2,1)} %bitcast.50) | data formatting | bytes 4194304 | tf_op jit(solution)/shard_map/gather | solution.py:24
  388.0 7.7 %select_bitcast_fusion.4 = (bf16[64,128,128]{2,1,0:T(8,128)(2,1)}, bf16[64,128,128]{2,1,0:T(8,128)(2,1)}, bf16[64,128,128]{2,1,0:T(8,128)(2,1)}, bf16[64,128,128...) fusion(bf16[128,128,64]{1,0,2:T(8,128)(2,1)} %copy.68, ...), kind=kLoop, calls=%fused_computation.22 | loop fusion | flops 6291456 | bytes 25198592 | tf_op jit(solution)/shard_map/jit(_where)/select_n | solution.py:26
  397.4 2.5 fusion.4
  406.3 3.3 collective-permute-start.2
  413.7 2.5 fusion
  420.9 2.2 copy.75
  429.0 2.5 fusion.8
  441.6 3.1 collective-permute-start.4
  448.6 2.8 collective-permute-done.4
  453.6 4.8 %psum.7 = f32[128]{0:T(128)S(1)} all-reduce(f32[128]{0:T(128)S(1)} %fusion.36), channel_id=1, replica_groups=mesh['seq'=16,'head'=2] {'head'}, use_global_device_ids=true, to_apply=%region_20.21 | all-reduce | flops 128 | bytes 1024 | tf_op jit(solution)/shard_map/psum | solution.py:94
  (105 shorter events, 41.2 us)
Async XLA Ops:
  0.0 396.2 %collective-permute-start.1 = (bf16[128,1024]{1,0:T(8,128)(2,1)}, bf16[128,1024]{1,0:T(8,128)(2,1)S(1)}, u32[]{:S(2)}, u32[]{:S(2)}) collective-permute-start(bf16[128,1024]{1,0:T(8,128)(2,1)} %param.7), channel_id=1, source_target_pairs={{0,2},{2,4},{4,6},{6,8},{8,10},{10,12},{12,14},{14,16},{16,18},{18... | collective-permute-start | bytes 786440 | tf_op jit(solution)/shard_map/ppermute | solution.py:14
  3.1 406.5 %collective-permute-start = (bf16[128,1024]{1,0:T(8,128)(2,1)}, bf16[128,1024]{1,0:T(8,128)(2,1)}, u32[]{:S(2)}, u32[]{:S(2)}) collective-permute-start(bf16[128,1024]{1,0:T(8,128)(2,1)} %param.6), channel_id=1, source_target_pairs={{0,2},{2,4},{4,6},{6,8},{8,10},{10,12},{12,14},{14,16},{16,18},{18... | collective-permute-start | bytes 786440 | tf_op jit(solution)/shard_map/ppermute | solution.py:14
  6.2 416.9 %collective-permute-start.3 = (bf16[128,1024]{1,0:T(8,128)(2,1)}, bf16[128,1024]{1,0:T(8,128)(2,1)}, u32[]{:S(2)}, u32[]{:S(2)}) collective-permute-start(bf16[128,1024]{1,0:T(8,128)(2,1)} %param.8), channel_id=1, source_target_pairs={{0,2},{2,4},{4,6},{6,8},{8,10},{10,12},{12,14},{14,16},{16,18},{18... | collective-permute-start | bytes 786440 | tf_op jit(solution)/shard_map/ppermute | solution.py:14
  388.0 7.7 %copy-start.11 = (s32[32]{0:T(128)S(1)}, s32[32]{0:T(128)}, u32[]{:S(2)}) copy-start(s32[32]{0:T(128)} %param.10) | copy-start | bytes 388
  388.0 8.0 %copy-start.10 = (bf16[1024]{0:T(1024)(128)(2,1)S(1)}, bf16[1024]{0:T(1024)(128)(2,1)}, u32[]{:S(2)}) copy-start(bf16[1024]{0:T(1024)(128)(2,1)} %param.11) | copy-start | bytes 6148
  388.0 8.2 %copy-start.7 = (bf16[128,1024]{1,0:T(8,128)(2,1)S(1)}, bf16[128,1024]{1,0:T(8,128)(2,1)}, u32[]{:S(2)}) copy-start(bf16[128,1024]{1,0:T(8,128)(2,1)} %param.7) | copy-start | bytes 786436
  395.7 1.7 copy-start.2
  403.8 5.8 %copy-start.8 = (bf16[128,1024]{1,0:T(8,128)(2,1)S(1)}, bf16[128,1024]{1,0:T(8,128)(2,1)}, u32[]{:S(2)}) copy-start(bf16[128,1024]{1,0:T(8,128)(2,1)} %param.6) | copy-start | bytes 786436
  404.9 8.8 %copy-start.1 = (bf16[64,128,128]{2,1,0:T(8,128)(2,1)S(1)}, bf16[64,128,128]{2,1,0:T(8,128)(2,1)}, u32[]{:S(2)}) copy-start(bf16[64,128,128]{2,1,0:T(8,128)(2,1)} %get-tuple-element.17) | copy-start | bytes 6291460
  406.3 38.5 %collective-permute-start.2 = (bf16[1024,128]{0,1:T(8,128)(2,1)S(1)}, bf16[1024,128]{0,1:T(8,128)(2,1)S(1)}, u32[]{:S(2)}, u32[]{:S(2)}) collective-permute-start(bf16[1024,128]{0,1:T(8,128)(2,1)S(1)} %multiply_convert_fusion.1), channel_id=1, source_target_pairs={{0,2},{2,4},{4,6},{6,8},{8,10},{10,12},{12,14},{14,16},{16,18},{18... | collective-permute-start | bytes 786440 | tf_op jit(solution)/shard_map/ppermute | solution.py:14
  419.8 3.3 copy-start.9
  420.9 8.1 %copy-start = (bf16[64,128,128]{2,1,0:T(8,128)(2,1)S(1)}, bf16[64,128,128]{2,1,0:T(8,128)(2,1)}, u32[]{:S(2)}) copy-start(bf16[64,128,128]{2,1,0:T(8,128)(2,1)} %get-tuple-element.19) | copy-start | bytes 6291460
  435.1 5.4 %copy-start.3 = (bf16[1024,256]{0,1:T(8,128)(2,1)S(1)}, bf16[1024,256]{0,1:T(8,128)(2,1)}, u32[]{:S(2)}) copy-start(bf16[1024,256]{0,1:T(8,128)(2,1)} %maximum_bitcast_fusion.2) | copy-start | bytes 1572868
  436.4 4.1 copy-start.6
  436.4 8.3 %copy-start.4 = (f32[1024,128]{0,1:T(8,128)S(1)}, f32[1024,128]{0,1:T(8,128)}, u32[]{:S(2)}) copy-start(f32[1024,128]{0,1:T(8,128)} %copy.74) | copy-start | bytes 1572868
  436.4 8.3 %copy-start.5 = (f32[1024,128]{0,1:T(8,128)S(1)}, f32[1024,128]{0,1:T(8,128)}, u32[]{:S(2)}) copy-start(f32[1024,128]{0,1:T(8,128)} %copy.75) | copy-start | bytes 1572868
  441.6 9.7 %collective-permute-start.4 = (bf16[1024,128]{0,1:T(8,128)(2,1)S(1)}, bf16[1024,128]{0,1:T(8,128)(2,1)S(1)}, u32[]{:S(2)}, u32[]{:S(2)}) collective-permute-start(bf16[1024,128]{0,1:T(8,128)(2,1)S(1)} %multiply_convert_fusion), channel_id=1, source_target_pairs={{0,2},{2,4},{4,6},{6,8},{8,10},{10,12},{12,14},{14,16},{16,18},{18... | collective-permute-start | bytes 786440 | tf_op jit(solution)/shard_map/ppermute | solution.py:14
where the time goes:
time: 461 us; the launch traced here: 460 us
  local copies, waits for them, and re-layouts  409 us (89%)
  starting transfers between devices  15.8 us (3%)
  other arithmetic  15.5 us (3%)
  matrix products  11.6 us (3%)
  blocking collectives  4.84 us (1%)
    gather x6, local copies, waits for them, and re-layouts, banded_pair(): beyond = filter_rows[:, jnp.clip(lag_index + tap_count, 0, tap_count - 1)]  189 us
    gather x6, local copies, waits for them, and re-layouts, banded_pair(): within = filter_rows[:, jnp.clip(lag_index, 0, tap_count - 1)]  188 us
    ppermute x5, starting transfers between devices, passed_along(): lax.ppermute(value, axis, [(source, source + steps) for source in range(i...  15.8 us
  transfers between devices with their start and end apart: 5, of which 1 were waited for; matrix products, arithmetic and copies ran while one was open for 94% of the time, Pallas kernels for 0%

commit v1 on v0

v1 whole, which is shorter than its diff:
```python
import math

import jax
import jax.numpy as jnp
from jax import lax
from jax.experimental import pallas as pl
from jax.experimental.pallas import tpu as pltpu
from jax.sharding import PartitionSpec as P

HDIM = 128
TEAM = 4
VMEM = pltpu.VMEM
F32 = jnp.float32
BF16 = jnp.bfloat16


def kernel_call(body, outs, args, scratch=(), flops=0):
    spec = pl.BlockSpec(memory_space=VMEM)
    moved = sum(math.prod(a.shape) * a.dtype.itemsize for a in list(args) + list(outs))
    return pl.pallas_call(
        body,
        out_shape=outs,
        in_specs=[spec] * len(args),
        out_specs=[spec] * len(outs),
        scratch_shapes=list(scratch),
        compiler_params=pltpu.CompilerParams(vmem_limit_bytes=48 * 1024 * 1024),
        cost_estimate=pl.CostEstimate(flops=flops, bytes_accessed=moved, transcendentals=0),
    )(*args)


def place():
    return lax.rem(lax.axis_index("seq"), TEAM)


def cut_parts(arrays):
    tokens, channels = arrays[0].shape
    share = channels // TEAM
    count = len(arrays)

    def body(*refs):
        ins, outs = refs[:count], refs[count:]
        me = place()
        for step in range(TEAM):
            first = pl.multiple_of(lax.bitwise_xor(me, step) * share, share)
            for i, ref in enumerate(ins):
                outs[step][i * share : (i + 1) * share, :] = ref[:, pl.ds(first, share)].T

    outs = [jax.ShapeDtypeStruct((count * share, tokens), BF16)] * TEAM
    return kernel_call(body, outs, arrays)


def bands(row):
    taps = row.shape[1]
    turned = pltpu.roll(jnp.broadcast_to(row, (taps, taps)), 0, 1, stride=1, stride_axis=0)
    lag = lax.broadcasted_iota(jnp.int32, (taps, taps), 1) - lax.broadcasted_iota(
        jnp.int32, (taps, taps), 0
    )
    zero = jnp.zeros_like(turned)
    earlier = jnp.where(lag < 0, turned, zero).astype(BF16)
    current = jnp.where(lag >= 0, turned, zero).astype(BF16)
    return jnp.concatenate([earlier, current], 0)


def attend_head(q_cols, k_rows, v_cols, starts, key_shift):
    span, tokens = k_rows.shape[0], q_cols.shape[1]
    scores = jnp.dot(k_rows, q_cols, preferred_element_type=F32) * (1.0 / math.sqrt(HDIM))
    key_pos = lax.broadcasted_iota(jnp.int32, (span, tokens), 0) + key_shift
    query_pos = lax.broadcasted_iota(jnp.int32, (span, tokens), 1)
    allowed = (key_pos >= starts) & (key_pos <= query_pos)
    scores = jnp.where(allowed, scores, -1e30)
    weights = jnp.exp(scores - jnp.max(scores, axis=0, keepdims=True))
    totals = jnp.sum(weights, axis=0, keepdims=True)
    mixed = jnp.dot(v_cols, weights.astype(BF16), preferred_element_type=F32)
    return (mixed / totals).astype(BF16)


def gated(x_now, conv):
    return (x_now.astype(F32) * conv).astype(BF16)


def inner_part(q_parts, kv_parts, filters, starts):
    share, tokens = q_parts[0].shape
    _, groups, taps = filters.shape
    team_groups = groups // TEAM
    width = share // team_groups
    heads = share // HDIM

    def body(*refs):
        q_refs, kv_refs = refs[:TEAM], refs[TEAM : 2 * TEAM]
        filter_ref, starts_ref = refs[2 * TEAM : 2 * TEAM + 2]
        late_ref, raw_ref, q1_ref, k1_ref, v1_ref = refs[2 * TEAM + 2 : 2 * TEAM + 7]
        x_ref, y_ref = refs[2 * TEAM + 7 :]
        me = place()
        for step in range(TEAM):
            block = lax.bitwise_xor(me, step)
            x_ref[block, 0] = q_refs[step][...]
            x_ref[block, 1] = kv_refs[step][:share]
            x_ref[block, 2] = kv_refs[step][share:]
        raw_ref[...] = x_ref[0]
        for part in range(3):
            first = pl.multiple_of(me * team_groups, team_groups)
            rows = filter_ref[part, pl.ds(first, team_groups), :].astype(F32)
            for group in range(team_groups):
                at = slice(group * width, (group + 1) * width)
                band = bands(rows[group : group + 1])
                left = jnp.concatenate(
                    [
                        jnp.concatenate([x_ref[b - 1, part, at], x_ref[b, part, at]], 1)
                        for b in range(1, TEAM)
                    ],
                    0,
                )
                conv = jnp.dot(left, band, preferred_element_type=F32)
                for b in range(1, TEAM):
                    y_ref[part, at, (b - 1) * tokens : b * tokens] = gated(
                        x_ref[b, part, at], conv[(b - 1) * width : b * width]
                    )
        q1_ref[...] = y_ref[0, :, :tokens]
        v1_ref[...] = y_ref[2, :, :tokens]
        for head in range(heads):
            at = slice(head * HDIM, (head + 1) * HDIM)
            keys = [y_ref[1, at, b * tokens : (b + 1) * tokens].T for b in range(TEAM - 1)]
            k1_ref[:, at] = keys[0]
            for b in range(2, TEAM):
                out = attend_head(
                    y_ref[0, at, (b - 1) * tokens : b * tokens],
                    jnp.concatenate([keys[b - 2], keys[b - 1]], 0),
                    y_ref[2, at, (b - 2) * tokens : b * tokens],
                    starts_ref[b : b + 1, :],
                    -tokens,
                )
                late_ref[b - 2, :, at] = out.T

    sds = jax.ShapeDtypeStruct
    outs = [
        sds((TEAM - 2, tokens, share), BF16),
        sds((3, share, tokens), BF16),
        sds((share, tokens), BF16),
        sds((tokens, share), BF16),
        sds((share, tokens), BF16),
    ]
    scratch = [
        VMEM((TEAM, 3, share, tokens), BF16),
        VMEM((3, share, (TEAM - 1) * tokens), BF16),
    ]
    flops = 2 * 3 * share * tokens * 2 * tokens * 4
    return kernel_call(
        body, outs, list(q_parts) + list(kv_parts) + [filters, starts], scratch, flops
    )


def rim_part(rim_q, rim_kv, raw, q1, k1, v1, late, filters, starts):
    share, tokens = rim_q.shape
    _, groups, taps = filters.shape
    team_groups = groups // TEAM
    width = share // team_groups
    heads = share // HDIM

    def body(*refs):
        rq_ref, rkv_ref, raw_ref, q1_ref, k1_ref, v1_ref, late_ref, filter_ref, starts_ref = refs[:9]
        outs = refs[9 : 9 + TEAM]
        y_ref, done_ref = refs[9 + TEAM :]
        me = place()
        for part in range(3):
            first = pl.multiple_of(me * team_groups, team_groups)
            rows = filter_ref[part, pl.ds(first, team_groups), :].astype(F32)
            for group in range(team_groups):
                at = slice(group * width, (group + 1) * width)
                band = bands(rows[group : group + 1])
                now = raw_ref[part, at]
                if part == 0:
                    left = jnp.concatenate([rq_ref[at], now], 1)
                    conv = jnp.dot(left, band, preferred_element_type=F32)
                    y_ref[0, at, tokens:] = gated(now, conv)
                    continue
                base = (part - 1) * share + group * width
                before = rkv_ref[base : base + width]
                further = rkv_ref[2 * share + base : 2 * share + base + width]
                left = jnp.concatenate(
                    [jnp.concatenate([further, before], 1), jnp.concatenate([before, now], 1)], 0
                )
                conv = jnp.dot(left, band, preferred_element_type=F32)
                y_ref[part, at, :tokens] = gated(before, conv[:width])
                y_ref[part, at, tokens:] = gated(now, conv[width:])
        done_ref[2:] = late_ref[...]
        for head in range(heads):
            at = slice(head * HDIM, (head + 1) * HDIM)
            k_far = y_ref[1, at, :tokens].T
            k_now = y_ref[1, at, tokens:].T
            out = attend_head(
                y_ref[0, at, tokens:],
                jnp.concatenate([k_far, k_now], 0),
                y_ref[2, at, :],
                starts_ref[0:1, :],
                -tokens,
            )
            done_ref[0, :, at] = out.T
            out = attend_head(
                q1_ref[at, :],
                jnp.concatenate([k_now, k1_ref[:, at]], 0),
                jnp.concatenate([y_ref[2, at, tokens:], v1_ref[at, :]], 1),
                starts_ref[1:2, :],
                -tokens,
            )
            done_ref[1, :, at] = out.T
        for step in range(TEAM):
            outs[step][...] = done_ref[lax.bitwise_xor(me, step)]

    outs = [jax.ShapeDtypeStruct((tokens, share), BF16)] * TEAM
    scratch = [
        VMEM((3, share, 2 * tokens), BF16),
        VMEM((TEAM, tokens, share), BF16),
    ]
    args = [rim_q, rim_kv, raw, q1, k1, v1, late, filters, starts]
    return kernel_call(body, outs, args, scratch)


def square_sums(parts):
    tokens, share = parts[0].shape

    def body(*refs):
        total = jnp.zeros((tokens, 1), F32)
        for ref in refs[:TEAM]:
            wide = ref[...].astype(F32)
            total = total + jnp.sum(wide * wide, axis=1, keepdims=True)
        refs[TEAM][...] = jnp.broadcast_to(total, (tokens, 128))

    return kernel_call(body, [jax.ShapeDtypeStruct((tokens, 128), F32)], parts)[0]


def scaled(parts, sums, gain, total_channels):
    tokens, share = parts[0].shape
    count = len(sums)

    def body(*refs):
        part_refs, sum_refs = refs[:TEAM], refs[TEAM : TEAM + count]
        gain_ref, out_ref = refs[TEAM + count :]
        me = place()
        total = sum_refs[0][...]
        for ref in sum_refs[1:]:
            total = total + ref[...]
        scale = lax.rsqrt(total / total_channels + 1e-06)
        scale = jnp.concatenate([scale] * (share // 128), 1)
        for step in range(TEAM):
            first = pl.multiple_of(lax.bitwise_xor(me, step) * share, share)
            wide = part_refs[step][...].astype(F32)
            wide = wide * scale * gain_ref[:, pl.ds(first, share)].astype(F32)
            out_ref[:, pl.ds(first, share)] = wide.astype(BF16)

    out = jax.ShapeDtypeStruct((tokens, TEAM * share), BF16)
    args = list(parts) + list(sums) + [gain.reshape(1, TEAM * share)]
    return kernel_call(body, [out], args)[0]


def swapped(value, step):
    count = lax.axis_size("seq")
    return lax.ppermute(value, "seq", [(i, i ^ step) for i in range(count)])


def onward(value):
    count = lax.axis_size("seq")
    return lax.ppermute(value, "seq", [(i, i + TEAM) for i in range(count - TEAM)])


def chosen(parts, block):
    return lax.select_n(lax.bitwise_xor(place(), block), *parts)


def document_starts(lengths, tokens):
    ends = jnp.cumsum(lengths)
    base = (lax.axis_index("seq") // TEAM) * (TEAM * tokens)
    pos = base + jnp.arange(TEAM * tokens, dtype=jnp.int32)
    begun = jnp.where(ends[:, None] <= pos[None, :], ends[:, None], 0)
    first = jnp.max(begun, axis=0).reshape(TEAM, tokens)
    block_base = base + tokens * jnp.arange(TEAM, dtype=jnp.int32)
    return first - block_base[:, None]


def per_device(q_in, k_in, v_in, filters, lengths, gain):
    tokens, channels = q_in.shape
    steps = (0, 3, 1, 2)
    kv_cut = cut_parts([k_in, v_in])
    q_cut = cut_parts([q_in])
    kv_parts = list(kv_cut)
    for step in steps[1:]:
        kv_parts[step] = swapped(kv_cut[step], step)
    q_parts = list(q_cut)
    for step in steps[1:]:
        q_parts[step] = swapped(q_cut[step], step)
    starts = document_starts(lengths, tokens)
    rim_kv = onward(jnp.concatenate([chosen(kv_parts, TEAM - 1), chosen(kv_parts, TEAM - 2)], 0))
    rim_q = onward(chosen(q_parts, TEAM - 1))
    late, raw, q1, k1, v1 = inner_part(q_parts, kv_parts, filters, starts)
    made = list(rim_part(rim_q, rim_kv, raw, q1, k1, v1, late, filters, starts))
    mine = list(made)
    for step in steps[1:]:
        mine[step] = swapped(made[step], step)
    own = square_sums(mine)
    head_count = lax.axis_size("head")
    if head_count == 2:
        sums = [own, lax.ppermute(own, "head", [(0, 1), (1, 0)])]
    else:
        sums = [lax.psum(own, "head")]
    return scaled(mine, sums, gain, channels * head_count)


def solution(mesh):
    placed = (
        P("seq", "head"),
        P("seq", "head"),
        P("seq", "head"),
        P(None, "head", None),
        P(),
        P("head"),
    )
    return jax.shard_map(
        per_device, mesh=mesh, in_specs=placed, out_specs=P("seq", "head"), check_vma=False
    )
```

time: 461 us -> 34.2 us (0.07)
  local copies, waits for them, and re-layouts: 409 us -> 2.66 us
  other arithmetic: 15.5 us -> 0.42 us
  matrix products: 11.6 us -> 0 us
  starting transfers between devices: 15.8 us -> 21 us
  blocking collectives: 4.84 us -> 0 us
    gather x12 -> x0, local copies, waits for them, and re-layouts: 377 us -> none  [the longest x6 189 us: banded_pair(): beyond = filter_rows[:, jnp.clip(lag_index + tap_count, 0, tap_count - 1)]]
    dot_general x19 -> x0, matrix products: 11.6 us -> none  [the longest x3 7.39 us: gated_conv(): jnp.einsum('grj,gji->gri', rows, stacked, preferred_element_type=jnp.floa...]
    reshape x9 -> x1, local copies, waits for them, and re-layouts: 10.7 us -> 0.01 us  [scaled(): args = list(parts) + list(sums) + [gain.reshape(1, TEAM * share)]]
    slice x10 -> x0, local copies, waits for them, and re-layouts: 7.71 us -> none  [the longest x6 3.73 us: gated_conv(): both[:, :, tap_count:].reshape(channels, span_len)[:, :tok_count]]
    select_n x1 -> x2, other arithmetic: 7.68 us -> 0.05 us  [chosen(): return lax.select_n(lax.bitwise_xor(place(), block), *parts)]
    unnamed x33 -> x12, local copies, waits for them, and re-layouts: 8.68 us -> 2.57 us
    ppermute x5 -> x12, starting transfers between devices: 15.8 us -> 21 us  [the longest x9 8.21 us: swapped(): return lax.ppermute(value, 'seq', [(i, i ^ step) for i in range(count)])]
    psum x1 -> x0, blocking collectives: 4.84 us -> none  [per_device(): total_squares = lax.psum(local_squares, 'head')]
  transfers between devices with their start and end apart: 5 -> 12, of which waited for: 1 -> 6; matrix products, arithmetic and copies ran while one was open for 94% -> 2% of each run, Pallas kernels for 0% -> 4%
where the time goes in v1:
time: 34.2 us; the launch traced here: 33.6 us
  starting transfers between devices  21 us (61%)
  waiting for transfers between devices  5.96 us (17%)
  Pallas kernels  3.44 us (10%)
  local copies, waits for them, and re-layouts  2.66 us (8%)
  other arithmetic  0.42 us (1%)
    ppermute x9, starting transfers between devices, swapped(): return lax.ppermute(value, 'seq', [(i, i ^ step) for i in range(count)])  8.21 us
    ppermute x2, starting transfers between devices, onward(): lax.ppermute(value, 'seq', [(i, i + TEAM) for i in range(count - TEAM)])  6.41 us
    ppermute x1, starting transfers between devices, per_device(): sums = [own, lax.ppermute(own, 'head', [(0, 1), (1, 0)])]  6.39 us
    ppermute x9, waiting for transfers between devices, swapped(): return lax.ppermute(value, 'seq', [(i, i ^ step) for i in range(count)])  3.47 us
    pallas_call x6, Pallas kernels, kernel_call(): pl.pallas_call(body, out_shape=outs, in_specs=[spec] * len(args), out_spe...  3.44 us
    unnamed x12, local copies, waits for them, and re-layouts  2.57 us
    ppermute x2, waiting for transfers between devices, onward(): lax.ppermute(value, 'seq', [(i, i + TEAM) for i in range(count - TEAM)])  1.6 us
    ppermute x1, waiting for transfers between devices, per_device(): sums = [own, lax.ppermute(own, 'head', [(0, 1), (1, 0)])]  0.89 us
  transfers between devices with their start and end apart: 12, of which 6 were waited for; matrix products, arithmetic and copies ran while one was open for 2% of the time, Pallas kernels for 4%

profile of v1, /device:TPU:9, one launch (start us, length us, event | category | flops | bytes accessed | tf_op | source)
XLA Modules:
  0.0 33.6 jit_solution(12663541522466222649)
XLA Ops:
  0.0 0.9 %copy-done = bf16[128,1024]{1,0:T(8,128)(2,1)S(1)} copy-done((bf16[128,1024]{1,0:T(8,128)(2,1)S(1)}, bf16[128,1024]{1,0:T(8,128)(2,1)}, u32[]{:S(2)}) %copy-start) | copy-done | bytes 262168
  1.0 0.9 %copy-done.1 = bf16[128,1024]{1,0:T(8,128)(2,1)S(1)} copy-done((bf16[128,1024]{1,0:T(8,128)(2,1)S(1)}, bf16[128,1024]{1,0:T(8,128)(2,1)}, u32[]{:S(2)}) %copy-start.1) | copy-done | bytes 262168
  1.9 0.2 shard_map.65
  2.1 1.3 %collective-permute-start.4 = (bf16[512,128]{1,0:T(8,128)(2,1)S(1)}, bf16[512,128]{1,0:T(8,128)(2,1)S(1)}, u32[]{:S(2)}, u32[]{:S(2)}) collective-permute-start(bf16[512,128]{1,0:T(8,128)(2,1)S(1)} %get-tuple-element.27), channel_id=1, source_target_pairs={{0,2},{2,0},{4,6},{6,4},{8,10},{10,8},{12,14},{14,12},{16,18},{18,... | collective-permute-start | bytes 393224 | tf_op jit(solution)/shard_map/ppermute | solution.py:257
  3.4 1.2 %collective-permute-start.5 = (bf16[512,128]{1,0:T(8,128)(2,1)S(1)}, bf16[512,128]{1,0:T(8,128)(2,1)S(1)}, u32[]{:S(2)}, u32[]{:S(2)}) collective-permute-start(bf16[512,128]{1,0:T(8,128)(2,1)S(1)} %get-tuple-element.28), channel_id=1, source_target_pairs={{0,4},{2,6},{4,0},{6,2},{8,12},{10,14},{12,8},{14,10},{16,20},{18,... | collective-permute-start | bytes 393224 | tf_op jit(solution)/shard_map/ppermute | solution.py:257
  4.6 0.2 collective-permute-start.6
  4.9 1.3 %collective-permute-start = (bf16[256,128]{1,0:T(8,128)(2,1)S(1)}, bf16[256,128]{1,0:T(8,128)(2,1)S(1)}, u32[]{:S(2)}, u32[]{:S(2)}) collective-permute-start(bf16[256,128]{1,0:T(8,128)(2,1)S(1)} %get-tuple-element.23), channel_id=1, source_target_pairs={{0,2},{2,0},{4,6},{6,4},{8,10},{10,8},{12,14},{14,12},{16,18},{18,... | collective-permute-start | bytes 196616 | tf_op jit(solution)/shard_map/ppermute | solution.py:257
  6.2 1.2 %collective-permute-start.1 = (bf16[256,128]{1,0:T(8,128)(2,1)S(1)}, bf16[256,128]{1,0:T(8,128)(2,1)S(1)}, u32[]{:S(2)}, u32[]{:S(2)}) collective-permute-start(bf16[256,128]{1,0:T(8,128)(2,1)S(1)} %get-tuple-element.24), channel_id=1, source_target_pairs={{0,4},{2,6},{4,0},{6,2},{8,12},{10,14},{12,8},{14,10},{16,20},{18,... | collective-permute-start | bytes 196616 | tf_op jit(solution)/shard_map/ppermute | solution.py:257
  7.5 0.7 %copy-done.5 = s32[32]{0:T(128)S(1)} copy-done((s32[32]{0:T(128)S(1)}, s32[32]{0:T(128)}, u32[]{:S(2)}) %copy-start.5) | copy-done | bytes 152
  8.5 0.3 collective-permute-start.2
  8.8 1.4 %collective-permute-done.6.refs_7_ = bf16[512,128]{1,0:T(8,128)(2,1)S(1)} collective-permute-done((bf16[512,128]{1,0:T(8,128)(2,1)S(1)}, bf16[512,128]{1,0:T(8,128)(2,1)S(1)}, u32[]{:S(2)}, u32[]{:S(2)}) %collective-permute-start.6) | collective-permute-done | bytes 131104 | tf_op jit(solution)/shard_map/ppermute | solution.py:257
  10.2 3.2 %collective-permute-start.7 = (bf16[1024,128]{1,0:T(8,128)(2,1)S(1)}, bf16[1024,128]{1,0:T(8,128)(2,1)S(1)}, u32[]{:S(2)}, u32[]{:S(2)}) collective-permute-start(bf16[1024,128]{1,0:T(8,128)(2,1)S(1)} %pad_maximum_fusion), channel_id=1, source_target_pairs={{0,8},{2,10},{4,12},{6,14},{8,16},{10,18},{12,20},{14,22},{16,24},... | collective-permute-start | bytes 786440 | tf_op jit(solution)/shard_map/ppermute | solution.py:262
  13.5 3.2 %collective-permute-start.3 = (bf16[256,128]{1,0:T(8,128)(2,1)S(1)}, bf16[256,128]{1,0:T(8,128)(2,1)S(1)}, u32[]{:S(2)}, u32[]{:S(2)}) collective-permute-start(bf16[256,128]{1,0:T(8,128)(2,1)S(1)} %select_select_fusion.2), channel_id=1, source_target_pairs={{0,8},{2,10},{4,12},{6,14},{8,16},{10,18},{12,20},{14,22},{16,24},... | collective-permute-start | bytes 196616 | tf_op jit(solution)/shard_map/ppermute | solution.py:262
  16.8 1.1 %shard_map.66 = (bf16[2,128,256]{2,1,0:T(8,128)(2,1)S(1)}, bf16[3,256,128]{2,1,0:T(8,128)(2,1)S(1)}, bf16[256,128]{1,0:T(8,128)(2,1)S(1)}, bf16[128,256]{1,0:T(8,128)(2,1)S(1)}, bf16[256,128]{1,0:T(8,128)(2,1)S(1)}) custom-call(bf16[256,128]{1,0:T(8,128)(2,1)S(1)} %get-tuple-element.22.refs_0_, bf16[256,128]{1,0:T(8,128)(2,1)S(1)} %collective-permute-done.refs_1_, ...), custom_call_target="tpu_custom_call" | custom-call | flops 201326592 | bytes 1361920 | tf_op jit(solution)/shard_map/pallas_call | solution.py:20
  17.9 1.6 %collective-permute-done.3.refs_0_ = bf16[256,128]{1,0:T(8,128)(2,1)S(1)} collective-permute-done((bf16[256,128]{1,0:T(8,128)(2,1)S(1)}, bf16[256,128]{1,0:T(8,128)(2,1)S(1)}, u32[]{:S(2)}, u32[]{:S(2)}) %collective-permute-start.3) | collective-permute-done | bytes 65568 | tf_op jit(solution)/shard_map/ppermute | solution.py:262
  19.5 1.1 %shard_map.67 = (bf16[128,256]{1,0:T(8,128)(2,1)S(1)}, bf16[128,256]{1,0:T(8,128)(2,1)S(1)}, bf16[128,256]{1,0:T(8,128)(2,1)S(1)}, bf16[128,256]{1,0:T(8,128)(2,1)S(1)}) custom-call(bf16[256,128]{1,0:T(8,128)(2,1)S(1)} %collective-permute-done.3.refs_0_, bf16[1024,128]{1,0:T(8,128)(2,1)S(1)} %collective-permute-done.7.refs_1_, ...), custom_call_target="tpu_custom_call" | custom-call | bytes 1165312 | tf_op jit(solution)/shard_map/pallas_call | solution.py:20
  20.6 1.1 %collective-permute-start.10 = (bf16[128,256]{1,0:T(8,128)(2,1)S(1)}, bf16[128,256]{1,0:T(8,128)(2,1)S(1)}, u32[]{:S(2)}, u32[]{:S(2)}) collective-permute-start(bf16[128,256]{1,0:T(8,128)(2,1)S(1)} %get-tuple-element.38), channel_id=1, source_target_pairs={{0,6},{2,4},{4,2},{6,0},{8,14},{10,12},{12,10},{14,8},{16,22},{18,... | collective-permute-start | bytes 196616 | tf_op jit(solution)/shard_map/ppermute | solution.py:257
  21.7 0.5 %collective-permute-start.8 = (bf16[128,256]{1,0:T(8,128)(2,1)S(1)}, bf16[128,256]{1,0:T(8,128)(2,1)S(1)}, u32[]{:S(2)}, u32[]{:S(2)}) collective-permute-start(bf16[128,256]{1,0:T(8,128)(2,1)S(1)} %get-tuple-element.36), channel_id=1, source_target_pairs={{0,2},{2,0},{4,6},{6,4},{8,10},{10,8},{12,14},{14,12},{16,18},{18,... | collective-permute-start | bytes 196616 | tf_op jit(solution)/shard_map/ppermute | solution.py:257
  22.1 1.2 %collective-permute-start.9 = (bf16[128,256]{1,0:T(8,128)(2,1)S(1)}, bf16[128,256]{1,0:T(8,128)(2,1)S(1)}, u32[]{:S(2)}, u32[]{:S(2)}) collective-permute-start(bf16[128,256]{1,0:T(8,128)(2,1)S(1)} %get-tuple-element.37), channel_id=1, source_target_pairs={{0,4},{2,6},{4,0},{6,2},{8,12},{10,14},{12,8},{14,10},{16,20},{18,... | collective-permute-start | bytes 196616 | tf_op jit(solution)/shard_map/ppermute | solution.py:257
  23.3 1.4 %collective-permute-done.10.refs_3_ = bf16[128,256]{1,0:T(8,128)(2,1)S(1)} collective-permute-done((bf16[128,256]{1,0:T(8,128)(2,1)S(1)}, bf16[128,256]{1,0:T(8,128)(2,1)S(1)}, u32[]{:S(2)}, u32[]{:S(2)}) %collective-permute-start.10) | collective-permute-done | bytes 65568 | tf_op jit(solution)/shard_map/ppermute | solution.py:257
  24.8 0.6 %collective-permute-done.9.refs_2_ = bf16[128,256]{1,0:T(8,128)(2,1)S(1)} collective-permute-done((bf16[128,256]{1,0:T(8,128)(2,1)S(1)}, bf16[128,256]{1,0:T(8,128)(2,1)S(1)}, u32[]{:S(2)}, u32[]{:S(2)}) %collective-permute-start.9) | collective-permute-done | bytes 65568 | tf_op jit(solution)/shard_map/ppermute | solution.py:257
  25.5 6.4 %collective-permute-start.11 = (f32[128,128]{1,0:T(8,128)S(1)}, f32[128,128]{1,0:T(8,128)S(1)}, u32[]{:S(2)}, u32[]{:S(2)}) collective-permute-start(f32[128,128]{1,0:T(8,128)S(1)} %shard_map.68.refs_4_), channel_id=1, source_target_pairs={{0,1},{1,0},{2,3},{3,2},{4,5},{5,4},{6,7},{7,6},{8,9},{9,8},{10,11... | collective-permute-start | bytes 196616 | tf_op jit(solution)/shard_map/ppermute | solution.py:301
  31.9 0.9 %collective-permute-done.11.refs_5_ = f32[128,128]{1,0:T(8,128)S(1)} collective-permute-done((f32[128,128]{1,0:T(8,128)S(1)}, f32[128,128]{1,0:T(8,128)S(1)}, u32[]{:S(2)}, u32[]{:S(2)}) %collective-permute-start.11) | collective-permute-done | bytes 65568 | tf_op jit(solution)/shard_map/ppermute | solution.py:301
  32.8 0.8 %shard_map.69 = bf16[128,1024]{1,0:T(8,128)(2,1)} custom-call(bf16[128,256]{1,0:T(8,128)(2,1)S(1)} %get-tuple-element.35.refs_0_, bf16[128,256]{1,0:T(8,128)(2,1)S(1)} %collective-permute-done.8.refs_1_, bf16[128,256]{1,0:T(8,128)(2,1)S(1)} %collective-permute-done.9.refs_2_, bf16[128,256]{1,0:T(8,128)(2,1)S(1)} %collective-permute-done.10.refs_3_, ...), custom_call_target="tpu_custom_call" | custom-call | bytes 657408 | tf_op jit(solution)/shard_map/pallas_call | solution.py:20
  (29 shorter events, 0.9 us)
Async XLA Ops:
  0.0 0.9 %copy-start = (bf16[128,1024]{1,0:T(8,128)(2,1)S(1)}, bf16[128,1024]{1,0:T(8,128)(2,1)}, u32[]{:S(2)}) copy-start(bf16[128,1024]{1,0:T(8,128)(2,1)} %refs_0_.3) | copy-start | bytes 786436
  1.0 0.9 %copy-start.1 = (bf16[128,1024]{1,0:T(8,128)(2,1)S(1)}, bf16[128,1024]{1,0:T(8,128)(2,1)}, u32[]{:S(2)}) copy-start(bf16[128,1024]{1,0:T(8,128)(2,1)} %refs_1_.1) | copy-start | bytes 786436
  1.9 2.9 %copy-start.2 = (bf16[128,1024]{1,0:T(8,128)(2,1)S(1)}, bf16[128,1024]{1,0:T(8,128)(2,1)}, u32[]{:S(2)}) copy-start(bf16[128,1024]{1,0:T(8,128)(2,1)} %refs_0_.2) | copy-start | bytes 786436
  2.1 6.4 %collective-permute-start.4 = (bf16[512,128]{1,0:T(8,128)(2,1)S(1)}, bf16[512,128]{1,0:T(8,128)(2,1)S(1)}, u32[]{:S(2)}, u32[]{:S(2)}) collective-permute-start(bf16[512,128]{1,0:T(8,128)(2,1)S(1)} %get-tuple-element.27), channel_id=1, source_target_pairs={{0,2},{2,0},{4,6},{6,4},{8,10},{10,8},{12,14},{14,12},{16,18},{18,... | collective-permute-start | bytes 393224 | tf_op jit(solution)/shard_map/ppermute | solution.py:257
  3.4 5.4 %collective-permute-start.5 = (bf16[512,128]{1,0:T(8,128)(2,1)S(1)}, bf16[512,128]{1,0:T(8,128)(2,1)S(1)}, u32[]{:S(2)}, u32[]{:S(2)}) collective-permute-start(bf16[512,128]{1,0:T(8,128)(2,1)S(1)} %get-tuple-element.28), channel_id=1, source_target_pairs={{0,4},{2,6},{4,0},{6,2},{8,12},{10,14},{12,8},{14,10},{16,20},{18,... | collective-permute-start | bytes 393224 | tf_op jit(solution)/shard_map/ppermute | solution.py:257
  4.6 5.5 %collective-permute-start.6 = (bf16[512,128]{1,0:T(8,128)(2,1)S(1)}, bf16[512,128]{1,0:T(8,128)(2,1)S(1)}, u32[]{:S(2)}, u32[]{:S(2)}) collective-permute-start(bf16[512,128]{1,0:T(8,128)(2,1)S(1)} %get-tuple-element.29), channel_id=1, source_target_pairs={{0,6},{2,4},{4,2},{6,0},{8,14},{10,12},{12,10},{14,8},{16,22},{18,... | collective-permute-start | bytes 393224 | tf_op jit(solution)/shard_map/ppermute | solution.py:257
  4.9 8.5 %collective-permute-start = (bf16[256,128]{1,0:T(8,128)(2,1)S(1)}, bf16[256,128]{1,0:T(8,128)(2,1)S(1)}, u32[]{:S(2)}, u32[]{:S(2)}) collective-permute-start(bf16[256,128]{1,0:T(8,128)(2,1)S(1)} %get-tuple-element.23), channel_id=1, source_target_pairs={{0,2},{2,0},{4,6},{6,4},{8,10},{10,8},{12,14},{14,12},{16,18},{18,... | collective-permute-start | bytes 196616 | tf_op jit(solution)/shard_map/ppermute | solution.py:257
  6.2 7.2 %collective-permute-start.1 = (bf16[256,128]{1,0:T(8,128)(2,1)S(1)}, bf16[256,128]{1,0:T(8,128)(2,1)S(1)}, u32[]{:S(2)}, u32[]{:S(2)}) collective-permute-start(bf16[256,128]{1,0:T(8,128)(2,1)S(1)} %get-tuple-element.24), channel_id=1, source_target_pairs={{0,4},{2,6},{4,0},{6,2},{8,12},{10,14},{12,8},{14,10},{16,20},{18,... | collective-permute-start | bytes 196616 | tf_op jit(solution)/shard_map/ppermute | solution.py:257
  7.5 0.7 %copy-start.5 = (s32[32]{0:T(128)S(1)}, s32[32]{0:T(128)}, u32[]{:S(2)}) copy-start(s32[32]{0:T(128)} %param.10) | copy-start | bytes 388
  8.5 5.0 %collective-permute-start.2 = (bf16[256,128]{1,0:T(8,128)(2,1)S(1)}, bf16[256,128]{1,0:T(8,128)(2,1)S(1)}, u32[]{:S(2)}, u32[]{:S(2)}) collective-permute-start(bf16[256,128]{1,0:T(8,128)(2,1)S(1)} %get-tuple-element.25), channel_id=1, source_target_pairs={{0,6},{2,4},{4,2},{6,0},{8,14},{10,12},{12,10},{14,8},{16,22},{18,... | collective-permute-start | bytes 196616 | tf_op jit(solution)/shard_map/ppermute | solution.py:257
  10.2 9.3 %collective-permute-start.7 = (bf16[1024,128]{1,0:T(8,128)(2,1)S(1)}, bf16[1024,128]{1,0:T(8,128)(2,1)S(1)}, u32[]{:S(2)}, u32[]{:S(2)}) collective-permute-start(bf16[1024,128]{1,0:T(8,128)(2,1)S(1)} %pad_maximum_fusion), channel_id=1, source_target_pairs={{0,8},{2,10},{4,12},{6,14},{8,16},{10,18},{12,20},{14,22},{16,24},... | collective-permute-start | bytes 786440 | tf_op jit(solution)/shard_map/ppermute | solution.py:262
  13.4 3.3 %copy-start.3 = (bf16[3,64,128]{2,1,0:T(8,128)(2,1)S(1)}, bf16[3,64,128]{2,1,0:T(8,128)(2,1)}, u32[]{:S(2)}) copy-start(bf16[3,64,128]{2,1,0:T(8,128)(2,1)} %refs_7_.1) | copy-start | bytes 147460
  13.5 6.0 %collective-permute-start.3 = (bf16[256,128]{1,0:T(8,128)(2,1)S(1)}, bf16[256,128]{1,0:T(8,128)(2,1)S(1)}, u32[]{:S(2)}, u32[]{:S(2)}) collective-permute-start(bf16[256,128]{1,0:T(8,128)(2,1)S(1)} %select_select_fusion.2), channel_id=1, source_target_pairs={{0,8},{2,10},{4,12},{6,14},{8,16},{10,18},{12,20},{14,22},{16,24},... | collective-permute-start | bytes 196616 | tf_op jit(solution)/shard_map/ppermute | solution.py:262
  20.6 4.1 %collective-permute-start.10 = (bf16[128,256]{1,0:T(8,128)(2,1)S(1)}, bf16[128,256]{1,0:T(8,128)(2,1)S(1)}, u32[]{:S(2)}, u32[]{:S(2)}) collective-permute-start(bf16[128,256]{1,0:T(8,128)(2,1)S(1)} %get-tuple-element.38), channel_id=1, source_target_pairs={{0,6},{2,4},{4,2},{6,0},{8,14},{10,12},{12,10},{14,8},{16,22},{18,... | collective-permute-start | bytes 196616 | tf_op jit(solution)/shard_map/ppermute | solution.py:257
  21.7 3.1 %collective-permute-start.8 = (bf16[128,256]{1,0:T(8,128)(2,1)S(1)}, bf16[128,256]{1,0:T(8,128)(2,1)S(1)}, u32[]{:S(2)}, u32[]{:S(2)}) collective-permute-start(bf16[128,256]{1,0:T(8,128)(2,1)S(1)} %get-tuple-element.36), channel_id=1, source_target_pairs={{0,2},{2,0},{4,6},{6,4},{8,10},{10,8},{12,14},{14,12},{16,18},{18,... | collective-permute-start | bytes 196616 | tf_op jit(solution)/shard_map/ppermute | solution.py:257
  22.1 3.3 %collective-permute-start.9 = (bf16[128,256]{1,0:T(8,128)(2,1)S(1)}, bf16[128,256]{1,0:T(8,128)(2,1)S(1)}, u32[]{:S(2)}, u32[]{:S(2)}) collective-permute-start(bf16[128,256]{1,0:T(8,128)(2,1)S(1)} %get-tuple-element.37), channel_id=1, source_target_pairs={{0,4},{2,6},{4,0},{6,2},{8,12},{10,14},{12,8},{14,10},{16,20},{18,... | collective-permute-start | bytes 196616 | tf_op jit(solution)/shard_map/ppermute | solution.py:257
  25.4 6.5 %copy-start.4 = (bf16[1024]{0:T(1024)(128)(2,1)S(1)}, bf16[1024]{0:T(1024)(128)(2,1)}, u32[]{:S(2)}) copy-start(bf16[1024]{0:T(1024)(128)(2,1)} %param.11) | copy-start | bytes 6148
  25.5 7.3 %collective-permute-start.11 = (f32[128,128]{1,0:T(8,128)S(1)}, f32[128,128]{1,0:T(8,128)S(1)}, u32[]{:S(2)}, u32[]{:S(2)}) collective-permute-start(f32[128,128]{1,0:T(8,128)S(1)} %shard_map.68.refs_4_), channel_id=1, source_target_pairs={{0,1},{1,0},{2,3},{3,2},{4,5},{5,4},{6,7},{7,6},{8,9},{9,8},{10,11... | collective-permute-start | bytes 196616 | tf_op jit(solution)/shard_map/ppermute | solution.py:301

commit v2 on v1

v2 whole, which is shorter than its diff:
```python
import math

import jax
import jax.numpy as jnp
from jax import lax
from jax.experimental import pallas as pl
from jax.experimental.pallas import tpu as pltpu
from jax.sharding import PartitionSpec as P

HDIM = 128
TEAM = 2
VMEM = pltpu.VMEM
F32 = jnp.float32
BF16 = jnp.bfloat16


def kernel_call(body, outs, args, scratch=(), flops=0, spaces=None, out_spaces=None):
    spaces = spaces or [VMEM] * len(args)
    out_spaces = out_spaces or [VMEM] * len(outs)
    moved = sum(math.prod(a.shape) * a.dtype.itemsize for a in list(args) + list(outs))
    return pl.pallas_call(
        body,
        out_shape=outs,
        in_specs=[pl.BlockSpec(memory_space=space) for space in spaces],
        out_specs=[pl.BlockSpec(memory_space=space) for space in out_spaces],
        scratch_shapes=list(scratch),
        compiler_params=pltpu.CompilerParams(vmem_limit_bytes=40 * 1024 * 1024),
        cost_estimate=pl.CostEstimate(flops=flops, bytes_accessed=moved, transcendentals=0),
    )(*args)


def place():
    return lax.rem(lax.axis_index("seq"), TEAM)


def cut_halves(arrays, stay=True):
    tokens, channels = arrays[0].shape
    share = channels // TEAM
    count = len(arrays)

    def body(*refs):
        ins, outs = refs[:count], refs[count : count + TEAM]
        held, sems = refs[count + TEAM :]
        me = place()
        copies = []
        for step in (1, 0):
            first = pl.multiple_of(lax.bitwise_xor(me, step) * share, share)
            for i, ref in enumerate(ins):
                copy = pltpu.make_async_copy(
                    ref.at[:, pl.ds(first, share)], held.at[i, step], sems.at[i, step]
                )
                copy.start()
                copies.append((copy, i, step))
        for copy, i, step in copies:
            copy.wait()
            outs[step][i * share : (i + 1) * share, :] = held[i, step].T

    outs = [jax.ShapeDtypeStruct((count * share, tokens), BF16)] * TEAM
    scratch = [
        VMEM((count, TEAM, tokens, share), BF16),
        pltpu.SemaphoreType.DMA((count, TEAM)),
    ]
    if stay:
        arrays = [pltpu.with_memory_space_constraint(a, pltpu.HBM) for a in arrays]
    return kernel_call(body, outs, arrays, scratch, spaces=[pl.ANY] * count)


def bands(row):
    taps = row.shape[1]
    turned = pltpu.roll(jnp.broadcast_to(row, (taps, taps)), 0, 1, stride=1, stride_axis=0)
    lag = lax.broadcasted_iota(jnp.int32, (taps, taps), 1) - lax.broadcasted_iota(
        jnp.int32, (taps, taps), 0
    )
    zero = jnp.zeros_like(turned)
    earlier = jnp.where(lag < 0, turned, zero).astype(BF16)
    current = jnp.where(lag >= 0, turned, zero).astype(BF16)
    return jnp.concatenate([earlier, current], 0)


def filter_rows(filter_ref, part, me):
    team_groups = filter_ref.shape[1] // TEAM
    first = pl.multiple_of(me * team_groups, team_groups)
    return filter_ref[part, pl.ds(first, team_groups), :].astype(F32)


def attend_head(q_cols, k_rows, v_cols, starts):
    span, tokens = k_rows.shape[0], q_cols.shape[1]
    scores = jnp.dot(k_rows, q_cols, preferred_element_type=F32) * (1.0 / math.sqrt(HDIM))
    key_pos = lax.broadcasted_iota(jnp.int32, (span, tokens), 0) - tokens
    query_pos = lax.broadcasted_iota(jnp.int32, (span, tokens), 1)
    allowed = (key_pos >= starts) & (key_pos <= query_pos)
    scores = jnp.where(allowed, scores, -1e30)
    weights = jnp.exp(scores - jnp.max(scores, axis=0, keepdims=True))
    totals = jnp.sum(weights, axis=0, keepdims=True)
    mixed = jnp.dot(v_cols, weights.astype(BF16), preferred_element_type=F32)
    return (mixed / totals).astype(BF16)


def gated(x_now, conv):
    return (x_now.astype(F32) * conv).astype(BF16)


def second_conv(q_own, q_got, kv_own, kv_got, filters):
    share, tokens = q_own.shape
    team_groups = filters.shape[1] // TEAM
    width = share // team_groups

    def body(q_own_ref, q_got_ref, kv_own_ref, kv_got_ref, filter_ref, raw_ref, last_ref, q1_ref, k1_ref, v1_ref, x_ref, y_ref):
        me = place()
        other = 1 - me
        x_ref[me, 0] = q_own_ref[...]
        x_ref[me, 1] = kv_own_ref[:share]
        x_ref[me, 2] = kv_own_ref[share:]
        x_ref[other, 0] = q_got_ref[...]
        x_ref[other, 1] = kv_got_ref[:share]
        x_ref[other, 2] = kv_got_ref[share:]
        raw_ref[...] = x_ref[0]
        last_ref[...] = x_ref[1, 0]
        for part in range(3):
            rows = filter_rows(filter_ref, part, me)
            for group in range(team_groups):
                at = slice(group * width, (group + 1) * width)
                now = x_ref[1, part, at]
                left = jnp.concatenate([x_ref[0, part, at], now], 1)
                conv = jnp.dot(left, bands(rows[group : group + 1]), preferred_element_type=F32)
                y_ref[part, at] = gated(now, conv)
        q1_ref[...] = y_ref[0]
        v1_ref[...] = y_ref[2]
        for first in range(0, share, HDIM):
            k1_ref[:, first : first + HDIM] = y_ref[1, first : first + HDIM].T

    sds = jax.ShapeDtypeStruct
    outs = [
        sds((3, share, tokens), BF16),
        sds((share, tokens), BF16),
        sds((share, tokens), BF16),
        sds((tokens, share), BF16),
        sds((share, tokens), BF16),
    ]
    scratch = [VMEM((TEAM, 3, share, tokens), BF16), VMEM((3, share, tokens), BF16)]
    flops = 2 * 3 * share * tokens * 2 * tokens * 8
    return kernel_call(body, outs, [q_own, q_got, kv_own, kv_got, filters], scratch, flops)


def rim_keys(rim_own, rim_got, raw, q1, k1, v1, filters, starts):
    share, tokens = q1.shape
    team_groups = filters.shape[1] // TEAM
    width = share // team_groups

    def body(own_ref, got_ref, raw_ref, q1_ref, k1_ref, v1_ref, filter_ref, starts_ref, k_ref, v_ref, out_ref, rim_ref, y_ref):
        me = place()
        rim_ref[me] = own_ref[...]
        rim_ref[1 - me] = got_ref[...]
        for part in (1, 2):
            rows = filter_rows(filter_ref, part, me)
            for group in range(team_groups):
                at = slice(group * width, (group + 1) * width)
                base = (part - 1) * share + group * width
                further = rim_ref[0, base : base + width]
                before = rim_ref[1, base : base + width]
                now = raw_ref[part, at]
                left = jnp.concatenate(
                    [jnp.concatenate([further, before], 1), jnp.concatenate([before, now], 1)], 0
                )
                conv = jnp.dot(left, bands(rows[group : group + 1]), preferred_element_type=F32)
                far = gated(before, conv[:width])
                near = gated(now, conv[width:])
                if part == 1:
                    y_ref[at, :tokens] = far
                    y_ref[at, tokens:] = near
                else:
                    v_ref[at, :tokens] = far
                    v_ref[at, tokens:] = near
        for first in range(0, share, HDIM):
            at = slice(first, first + HDIM)
            k_ref[:tokens, at] = y_ref[at, :tokens].T
            near = y_ref[at, tokens:].T
            k_ref[tokens:, at] = near
            out = attend_head(
                q1_ref[at, :],
                jnp.concatenate([near, k1_ref[:, at]], 0),
                jnp.concatenate([v_ref[at, tokens:], v1_ref[at, :]], 1),
                starts_ref[1:2, :],
            )
            out_ref[:, at] = out.T

    sds = jax.ShapeDtypeStruct
    outs = [
        sds((2 * tokens, share), BF16),
        sds((share, 2 * tokens), BF16),
        sds((tokens, share), BF16),
    ]
    scratch = [VMEM((TEAM, 2 * share, tokens), BF16), VMEM((share, 2 * tokens), BF16)]
    args = [rim_own, rim_got, raw, q1, k1, v1, filters, starts]
    return kernel_call(body, outs, args, scratch, 2 * 2 * share * tokens * 2 * tokens * 8)


def first_attention(rim_q, raw, keys, values, second, filters, starts):
    share, tokens = rim_q.shape
    team_groups = filters.shape[1] // TEAM
    width = share // team_groups

    def body(rim_ref, raw_ref, k_ref, v_ref, second_ref, filter_ref, starts_ref, keep_ref, send_ref, y_ref, out_ref):
        me = place()
        rows = filter_rows(filter_ref, 0, me)
        for group in range(team_groups):
            at = slice(group * width, (group + 1) * width)
            now = raw_ref[0, at]
            left = jnp.concatenate([rim_ref[at], now], 1)
            conv = jnp.dot(left, bands(rows[group : group + 1]), preferred_element_type=F32)
            y_ref[at] = gated(now, conv)
        for first in range(0, share, HDIM):
            at = slice(first, first + HDIM)
            out = attend_head(y_ref[at], k_ref[:, at], v_ref[at, :], starts_ref[0:1, :])
            out_ref[0, :, at] = out.T
        out_ref[1] = second_ref[...]
        keep_ref[...] = out_ref[me]
        send_ref[...] = out_ref[1 - me]

    outs = [jax.ShapeDtypeStruct((tokens, share), BF16)] * 2
    scratch = [VMEM((share, tokens), BF16), VMEM((TEAM, tokens, share), BF16)]
    args = [rim_q, raw, keys, values, second, filters, starts]
    return kernel_call(body, outs, args, scratch, 2 * share * tokens * 2 * tokens * 8)


def square_sums(parts):
    tokens = parts[0].shape[0]

    def body(*refs):
        total = jnp.zeros((tokens, 1), F32)
        for ref in refs[:-1]:
            wide = ref[...].astype(F32)
            total = total + jnp.sum(wide * wide, axis=1, keepdims=True)
        refs[-1][...] = jnp.broadcast_to(total, (tokens, 128))

    return kernel_call(body, [jax.ShapeDtypeStruct((tokens, 128), F32)], parts)[0]


def scaled(parts, sums, gain, total_channels):
    tokens, share = parts[0].shape
    count = len(sums)

    def body(*refs):
        part_refs, sum_refs = refs[:TEAM], refs[TEAM : TEAM + count]
        gain_ref, out_ref, held, sems = refs[TEAM + count :]
        me = place()
        total = sum_refs[0][...]
        for ref in sum_refs[1:]:
            total = total + ref[...]
        scale = lax.rsqrt(total / total_channels + 1e-06)
        piece = share // 2
        scale = jnp.concatenate([scale] * (piece // 128), 1)
        copies = []
        for step in range(TEAM):
            for cut in range(2):
                at = slice(cut * piece, (cut + 1) * piece)
                first = pl.multiple_of(lax.bitwise_xor(me, step) * share + cut * piece, piece)
                wide = part_refs[step][:, at].astype(F32)
                wide = wide * scale * gain_ref[:, pl.ds(first, piece)].astype(F32)
                held[step, cut] = wide.astype(BF16)
                copy = pltpu.make_async_copy(
                    held.at[step, cut], out_ref.at[:, pl.ds(first, piece)], sems.at[step, cut]
                )
                copy.start()
                copies.append(copy)
        for copy in copies:
            copy.wait()

    out = jax.ShapeDtypeStruct((tokens, TEAM * share), BF16)
    args = list(parts) + list(sums) + [gain.reshape(1, TEAM * share)]
    scratch = [
        VMEM((TEAM, 2, tokens, share // 2), BF16),
        pltpu.SemaphoreType.DMA((TEAM, 2)),
    ]
    return kernel_call(body, [out], args, scratch, out_spaces=[pltpu.HBM])[0]


def swapped(value):
    count = lax.axis_size("seq")
    return lax.ppermute(value, "seq", [(i, i ^ 1) for i in range(count)])


def onward(value):
    count = lax.axis_size("seq")
    return lax.ppermute(value, "seq", [(i, i + TEAM) for i in range(count - TEAM)])


def document_starts(lengths, tokens):
    ends = jnp.cumsum(lengths)
    base = (lax.axis_index("seq") // TEAM) * (TEAM * tokens)
    pos = base + jnp.arange(TEAM * tokens, dtype=jnp.int32)
    begun = jnp.where(ends[:, None] <= pos[None, :], ends[:, None], 0)
    first = jnp.max(begun, axis=0).reshape(TEAM, tokens)
    block_base = base + tokens * jnp.arange(TEAM, dtype=jnp.int32)
    return first - block_base[:, None]


def per_device(q_in, k_in, v_in, filters, lengths, gain):
    tokens, channels = q_in.shape
    kv_own, kv_other = cut_halves([k_in, v_in])
    half = kv_other.shape[0] // 2
    k_got = swapped(kv_other[:half])
    v_got = swapped(kv_other[half:])
    q_own, q_other = cut_halves([q_in], stay=False)
    q_other, k_got = lax.optimization_barrier((q_other, k_got))
    q_got = swapped(q_other)
    rim_own = onward(kv_own)
    kv_got = jnp.concatenate([k_got, v_got], 0)
    rim_got = onward(kv_got)
    starts = document_starts(lengths, tokens)
    raw, last_q, q1, k1, v1 = second_conv(q_own, q_got, kv_own, kv_got, filters)
    rim_q = onward(last_q)
    keys, values, second = rim_keys(rim_own, rim_got, raw, q1, k1, v1, filters, starts)
    keep, send = first_attention(rim_q, raw, keys, values, second, filters, starts)
    mine = [keep, swapped(send)]
    own = square_sums(mine)
    head_count = lax.axis_size("head")
    if head_count == 2:
        sums = [own, lax.ppermute(own, "head", [(0, 1), (1, 0)])]
    else:
        sums = [lax.psum(own, "head")]
    return scaled(mine, sums, gain, channels * head_count)


def solution(mesh):
    placed = (
        P("seq", "head"),
        P("seq", "head"),
        P("seq", "head"),
        P(None, "head", None),
        P(),
        P("head"),
    )
    return jax.shard_map(
        per_device, mesh=mesh, in_specs=placed, out_specs=P("seq", "head"), check_vma=False
    )
```

time: 34.2 us -> 31.7 us (0.927)
  the two profiles are of different devices: /device:TPU:9 before, /device:TPU:27 now
where the time goes in v2:
time: 31.7 us; the launch traced here: 31.4 us
  starting transfers between devices  15 us (47%)
  waiting for transfers between devices  9.49 us (30%)
  Pallas kernels  5.66 us (18%)
  local copies, waits for them, and re-layouts  0.81 us (3%)
  other arithmetic  0.35 us (1%)
    ppermute x3, starting transfers between devices, onward(): lax.ppermute(value, 'seq', [(i, i + TEAM) for i in range(count - TEAM)])  8.78 us
    pallas_call x7, Pallas kernels, kernel_call(): pl.pallas_call(body, out_shape=outs, in_specs=[pl.BlockSpec(memory_space=...  5.66 us
    ppermute x3, waiting for transfers between devices, onward(): lax.ppermute(value, 'seq', [(i, i + TEAM) for i in range(count - TEAM)])  4.33 us
    ppermute x4, waiting for transfers between devices, swapped(): return lax.ppermute(value, 'seq', [(i, i ^ 1) for i in range(count)])  4.27 us
    ppermute x1, starting transfers between devices, per_device(): sums = [own, lax.ppermute(own, 'head', [(0, 1), (1, 0)])]  3.83 us
    ppermute x4, starting transfers between devices, swapped(): return lax.ppermute(value, 'seq', [(i, i ^ 1) for i in range(count)])  2.35 us
    ppermute x1, waiting for transfers between devices, per_device(): sums = [own, lax.ppermute(own, 'head', [(0, 1), (1, 0)])]  0.89 us
    unnamed x9, local copies, waits for them, and re-layouts  0.68 us
  transfers between devices with their start and end apart: 8, of which 5 were waited for; matrix products, arithmetic and copies ran while one was open for 1% of the time, Pallas kernels for 8%

profile of v2, /device:TPU:27, one launch (start us, length us, event | category | flops | bytes accessed | tf_op | source)
XLA Modules:
  0.0 31.4 jit_solution(3010339395368952782)
XLA Ops:
  0.0 1.3 %shard_map.65 = (bf16[1024,128]{1,0:T(8,128)(2,1)S(1)}, bf16[1024,128]{1,0:T(8,128)(2,1)S(1)}) custom-call(bf16[128,1024]{1,0:T(8,128)(2,1)} %refs_0_.3, bf16[128,1024]{1,0:T(8,128)(2,1)} %refs_1_.1), custom_call_target="tpu_custom_call" | custom-call | bytes 1048576 | tf_op jit(solution)/shard_map/pallas_call | solution.py:21
  1.3 0.3 %collective-permute-start = (bf16[512,128]{1,0:T(8,128)(2,1)S(1)}, bf16[512,128]{1,0:T(8,128)(2,1)S(1)}, u32[]{:S(2)}, u32[]{:S(2)}) collective-permute-start(bf16[512,128]{1,0:T(8,128)(2,1)S(1)} %get-tuple-element.38), channel_id=1, source_target_pairs={{0,2},{2,0},{4,6},{6,4},{8,10},{10,8},{12,14},{14,12},{16,18},{18,... | collective-permute-start | bytes 393224 | tf_op jit(solution)/shard_map/ppermute | solution.py:280
  1.7 1.2 %collective-permute-start.2 = (bf16[512,128]{1,0:T(8,128)(2,1)S(1)}, bf16[512,128]{1,0:T(8,128)(2,1)S(1)}, u32[]{:S(2)}, u32[]{:S(2)}) collective-permute-start(bf16[512,128]{1,0:T(8,128)(2,1)S(1)} %get-tuple-element.37), channel_id=1, source_target_pairs={{0,2},{2,0},{4,6},{6,4},{8,10},{10,8},{12,14},{14,12},{16,18},{18,... | collective-permute-start | bytes 393224 | tf_op jit(solution)/shard_map/ppermute | solution.py:280
  2.9 3.1 %collective-permute-start.4 = (bf16[1024,128]{1,0:T(8,128)(2,1)S(1)}, bf16[1024,128]{1,0:T(8,128)(2,1)S(1)}, u32[]{:S(2)}, u32[]{:S(2)}) collective-permute-start(bf16[1024,128]{1,0:T(8,128)(2,1)S(1)} %get-tuple-element.25.kv_own_ref), channel_id=1, source_target_pairs={{0,4},{2,6},{4,8},{6,10},{8,12},{10,14},{12,16},{14,18},{16,20},{1... | collective-permute-start | bytes 786440 | tf_op jit(solution)/shard_map/ppermute | solution.py:285
  6.1 0.6 %copy-done.3 = s32[32]{0:T(128)S(1)} copy-done((s32[32]{0:T(128)S(1)}, s32[32]{0:T(128)}, u32[]{:S(2)}) %copy-start.3) | copy-done | bytes 152
  6.7 0.1 copy.9
  6.8 0.1 reduce
  7.0 0.1 select_reduce_fusion
  7.1 0.3 shard_map.64
  7.3 0.3 %collective-permute-start.1 = (bf16[512,128]{1,0:T(8,128)(2,1)S(1)}, bf16[512,128]{1,0:T(8,128)(2,1)S(1)}, u32[]{:S(2)}, u32[]{:S(2)}) collective-permute-start(bf16[512,128]{1,0:T(8,128)(2,1)S(1)} %get-tuple-element.24), channel_id=1, source_target_pairs={{0,2},{2,0},{4,6},{6,4},{8,10},{10,8},{12,14},{14,12},{16,18},{18,... | collective-permute-start | bytes 393224 | tf_op jit(solution)/shard_map/ppermute | solution.py:280
  7.7 0.9 %collective-permute-done.2 = bf16[512,128]{1,0:T(8,128)(2,1)S(1)} collective-permute-done((bf16[512,128]{1,0:T(8,128)(2,1)S(1)}, bf16[512,128]{1,0:T(8,128)(2,1)S(1)}, u32[]{:S(2)}, u32[]{:S(2)}) %collective-permute-start.2) | collective-permute-done | bytes 131104 | tf_op jit(solution)/shard_map/ppermute | solution.py:280
  8.6 3.1 %collective-permute-start.5 = (bf16[1024,128]{1,0:T(8,128)(2,1)S(1)}, bf16[1024,128]{1,0:T(8,128)(2,1)S(1)}, u32[]{:S(2)}, u32[]{:S(2)}) collective-permute-start(bf16[1024,128]{1,0:T(8,128)(2,1)S(1)} %constant_dynamic-update-slice_fusion.kv_got_ref), channel_id=1, source_target_pairs={{0,4},{2,6},{4,8},{6,10},{8,12},{10,14},{12,16},{14,18},{16,20},{1... | collective-permute-start | bytes 786440 | tf_op jit(solution)/shard_map/ppermute | solution.py:285
  11.8 1.1 %shard_map.66 = (bf16[3,512,128]{2,1,0:T(8,128)(2,1)S(1)}, bf16[512,128]{1,0:T(8,128)(2,1)S(1)}, bf16[512,128]{1,0:T(8,128)(2,1)S(1)}, bf16[128,512]{1,0:T(8,128)(2,1)S(1)}, bf16[512,128]{1,0:T(8,128)(2,1)S(1)}) custom-call(bf16[512,128]{1,0:T(8,128)(2,1)S(1)} %get-tuple-element.21.q_own_ref, bf16[512,128]{1,0:T(8,128)(2,1)S(1)} %collective-permute-done.1.q_got_ref, ...), custom_call_target="tpu_custom_call" | custom-call | flops 805306368 | bytes 1753088 | tf_op jit(solution)/shard_map/pallas_call | solution.py:21
  12.9 2.5 %collective-permute-start.3 = (bf16[512,128]{1,0:T(8,128)(2,1)S(1)}, bf16[512,128]{1,0:T(8,128)(2,1)S(1)}, u32[]{:S(2)}, u32[]{:S(2)}) collective-permute-start(bf16[512,128]{1,0:T(8,128)(2,1)S(1)} %get-tuple-element.27), channel_id=1, source_target_pairs={{0,4},{2,6},{4,8},{6,10},{8,12},{10,14},{12,16},{14,18},{16,20},{1... | collective-permute-start | bytes 393224 | tf_op jit(solution)/shard_map/ppermute | solution.py:285
  15.5 2.2 %collective-permute-done.5.got_ref = bf16[1024,128]{1,0:T(8,128)(2,1)S(1)} collective-permute-done((bf16[1024,128]{1,0:T(8,128)(2,1)S(1)}, bf16[1024,128]{1,0:T(8,128)(2,1)S(1)}, u32[]{:S(2)}, u32[]{:S(2)}) %collective-permute-start.5) | collective-permute-done | bytes 262176 | tf_op jit(solution)/shard_map/ppermute | solution.py:285
  17.6 1.2 %shard_map.67 = (bf16[256,512]{1,0:T(8,128)(2,1)S(1)}, bf16[512,256]{1,0:T(8,128)(2,1)S(1)}, bf16[128,512]{1,0:T(8,128)(2,1)S(1)}) custom-call(bf16[1024,128]{1,0:T(8,128)(2,1)S(1)} %collective-permute-done.4.own_ref, bf16[1024,128]{1,0:T(8,128)(2,1)S(1)} %collective-permute-done.5.got_ref, bf16[3,512,128]{2,1,0:T(8,128)(2,1)S(1)} %get-tuple-element.28.raw_ref, ...), custom_call_target="tpu_custom_call" | custom-call | flops 536870912 | bytes 2016256 | tf_op jit(solution)/shard_map/pallas_call | solution.py:21
  18.9 2.1 %collective-permute-done.3.rim_ref = bf16[512,128]{1,0:T(8,128)(2,1)S(1)} collective-permute-done((bf16[512,128]{1,0:T(8,128)(2,1)S(1)}, bf16[512,128]{1,0:T(8,128)(2,1)S(1)}, u32[]{:S(2)}, u32[]{:S(2)}) %collective-permute-start.3) | collective-permute-done | bytes 131104 | tf_op jit(solution)/shard_map/ppermute | solution.py:285
  21.0 0.9 %shard_map.68 = (bf16[128,512]{1,0:T(8,128)(2,1)S(1)}, bf16[128,512]{1,0:T(8,128)(2,1)S(1)}) custom-call(bf16[512,128]{1,0:T(8,128)(2,1)S(1)} %collective-permute-done.3.rim_ref, bf16[3,512,128]{2,1,0:T(8,128)(2,1)S(1)} %get-tuple-element.28.raw_ref, bf16[256,512]{1,0:T(8,128)(2,1)S(1)} %get-tuple-element.32.k_ref, ...), custom_call_target="tpu_custom_call" | custom-call | flops 268435456 | bytes 1491968 | tf_op jit(solution)/shard_map/pallas_call | solution.py:21
  21.9 0.5 %collective-permute-start.6 = (bf16[128,512]{1,0:T(8,128)(2,1)S(1)}, bf16[128,512]{1,0:T(8,128)(2,1)S(1)}, u32[]{:S(2)}, u32[]{:S(2)}) collective-permute-start(bf16[128,512]{1,0:T(8,128)(2,1)S(1)} %get-tuple-element.36), channel_id=1, source_target_pairs={{0,2},{2,0},{4,6},{6,4},{8,10},{10,8},{12,14},{14,12},{16,18},{18,... | collective-permute-start | bytes 393224 | tf_op jit(solution)/shard_map/ppermute | solution.py:280
  22.4 3.4 %collective-permute-done.6.refs_1_ = bf16[128,512]{1,0:T(8,128)(2,1)S(1)} collective-permute-done((bf16[128,512]{1,0:T(8,128)(2,1)S(1)}, bf16[128,512]{1,0:T(8,128)(2,1)S(1)}, u32[]{:S(2)}, u32[]{:S(2)}) %collective-permute-start.6) | collective-permute-done | bytes 131104 | tf_op jit(solution)/shard_map/ppermute | solution.py:280
  25.8 0.1 shard_map.69.refs_2_
  25.9 3.8 %collective-permute-start.7 = (f32[128,128]{1,0:T(8,128)S(1)}, f32[128,128]{1,0:T(8,128)S(1)}, u32[]{:S(2)}, u32[]{:S(2)}) collective-permute-start(f32[128,128]{1,0:T(8,128)S(1)} %shard_map.69.refs_2_), channel_id=1, source_target_pairs={{0,1},{1,0},{2,3},{3,2},{4,5},{5,4},{6,7},{7,6},{8,9},{9,8},{10,11... | collective-permute-start | bytes 196616 | tf_op jit(solution)/shard_map/ppermute | solution.py:319
  29.8 0.9 %collective-permute-done.7.refs_3_ = f32[128,128]{1,0:T(8,128)S(1)} collective-permute-done((f32[128,128]{1,0:T(8,128)S(1)}, f32[128,128]{1,0:T(8,128)S(1)}, u32[]{:S(2)}, u32[]{:S(2)}) %collective-permute-start.7) | collective-permute-done | bytes 65568 | tf_op jit(solution)/shard_map/ppermute | solution.py:319
  30.7 0.8 %shard_map.70 = bf16[128,1024]{1,0:T(8,128)(2,1)} custom-call(bf16[128,512]{1,0:T(8,128)(2,1)S(1)} %get-tuple-element.35.refs_0_, bf16[128,512]{1,0:T(8,128)(2,1)S(1)} %collective-permute-done.6.refs_1_, f32[128,128]{1,0:T(8,128)S(1)} %shard_map.69.refs_2_, f32[128,128]{1,0:T(8,128)S(1)} %collective-permute-done.7.refs_3_, bf16[1,1024]{1,0:T(2,128)(2,1)S(1)} %reshape.41.refs_4_), custom_call_target="tpu_custom_call" | custom-call | bytes 657408 | tf_op jit(solution)/shard_map/pallas_call | solution.py:21
  (18 shorter events, 0.2 us)
Async XLA Ops:
  1.3 5.8 %copy-start = (bf16[128,1024]{1,0:T(8,128)(2,1)S(1)}, bf16[128,1024]{1,0:T(8,128)(2,1)}, u32[]{:S(2)}) copy-start(bf16[128,1024]{1,0:T(8,128)(2,1)} %refs_0_.2) | copy-start | bytes 786436
  1.3 6.0 %collective-permute-start = (bf16[512,128]{1,0:T(8,128)(2,1)S(1)}, bf16[512,128]{1,0:T(8,128)(2,1)S(1)}, u32[]{:S(2)}, u32[]{:S(2)}) collective-permute-start(bf16[512,128]{1,0:T(8,128)(2,1)S(1)} %get-tuple-element.38), channel_id=1, source_target_pairs={{0,2},{2,0},{4,6},{6,4},{8,10},{10,8},{12,14},{14,12},{16,18},{18,... | collective-permute-start | bytes 393224 | tf_op jit(solution)/shard_map/ppermute | solution.py:280
  1.7 6.9 %collective-permute-start.2 = (bf16[512,128]{1,0:T(8,128)(2,1)S(1)}, bf16[512,128]{1,0:T(8,128)(2,1)S(1)}, u32[]{:S(2)}, u32[]{:S(2)}) collective-permute-start(bf16[512,128]{1,0:T(8,128)(2,1)S(1)} %get-tuple-element.37), channel_id=1, source_target_pairs={{0,2},{2,0},{4,6},{6,4},{8,10},{10,8},{12,14},{14,12},{16,18},{18,... | collective-permute-start | bytes 393224 | tf_op jit(solution)/shard_map/ppermute | solution.py:280
  2.9 12.6 %collective-permute-start.4 = (bf16[1024,128]{1,0:T(8,128)(2,1)S(1)}, bf16[1024,128]{1,0:T(8,128)(2,1)S(1)}, u32[]{:S(2)}, u32[]{:S(2)}) collective-permute-start(bf16[1024,128]{1,0:T(8,128)(2,1)S(1)} %get-tuple-element.25.kv_own_ref), channel_id=1, source_target_pairs={{0,4},{2,6},{4,8},{6,10},{8,12},{10,14},{12,16},{14,18},{16,20},{1... | collective-permute-start | bytes 786440 | tf_op jit(solution)/shard_map/ppermute | solution.py:285
  6.0 0.7 %copy-start.3 = (s32[32]{0:T(128)S(1)}, s32[32]{0:T(128)}, u32[]{:S(2)}) copy-start(s32[32]{0:T(128)} %param.10) | copy-start | bytes 388
  7.3 4.4 %collective-permute-start.1 = (bf16[512,128]{1,0:T(8,128)(2,1)S(1)}, bf16[512,128]{1,0:T(8,128)(2,1)S(1)}, u32[]{:S(2)}, u32[]{:S(2)}) collective-permute-start(bf16[512,128]{1,0:T(8,128)(2,1)S(1)} %get-tuple-element.24), channel_id=1, source_target_pairs={{0,2},{2,0},{4,6},{6,4},{8,10},{10,8},{12,14},{14,12},{16,18},{18,... | collective-permute-start | bytes 393224 | tf_op jit(solution)/shard_map/ppermute | solution.py:280
  7.7 4.1 %copy-start.1 = (bf16[3,64,128]{2,1,0:T(8,128)(2,1)S(1)}, bf16[3,64,128]{2,1,0:T(8,128)(2,1)}, u32[]{:S(2)}) copy-start(bf16[3,64,128]{2,1,0:T(8,128)(2,1)} %filter_ref.5) | copy-start | bytes 147460
  8.6 9.0 %collective-permute-start.5 = (bf16[1024,128]{1,0:T(8,128)(2,1)S(1)}, bf16[1024,128]{1,0:T(8,128)(2,1)S(1)}, u32[]{:S(2)}, u32[]{:S(2)}) collective-permute-start(bf16[1024,128]{1,0:T(8,128)(2,1)S(1)} %constant_dynamic-update-slice_fusion.kv_got_ref), channel_id=1, source_target_pairs={{0,4},{2,6},{4,8},{6,10},{8,12},{10,14},{12,16},{14,18},{16,20},{1... | collective-permute-start | bytes 786440 | tf_op jit(solution)/shard_map/ppermute | solution.py:285
  12.9 8.1 %collective-permute-start.3 = (bf16[512,128]{1,0:T(8,128)(2,1)S(1)}, bf16[512,128]{1,0:T(8,128)(2,1)S(1)}, u32[]{:S(2)}, u32[]{:S(2)}) collective-permute-start(bf16[512,128]{1,0:T(8,128)(2,1)S(1)} %get-tuple-element.27), channel_id=1, source_target_pairs={{0,4},{2,6},{4,8},{6,10},{8,12},{10,14},{12,16},{14,18},{16,20},{1... | collective-permute-start | bytes 393224 | tf_op jit(solution)/shard_map/ppermute | solution.py:285
  21.9 3.9 %collective-permute-start.6 = (bf16[128,512]{1,0:T(8,128)(2,1)S(1)}, bf16[128,512]{1,0:T(8,128)(2,1)S(1)}, u32[]{:S(2)}, u32[]{:S(2)}) collective-permute-start(bf16[128,512]{1,0:T(8,128)(2,1)S(1)} %get-tuple-element.36), channel_id=1, source_target_pairs={{0,2},{2,0},{4,6},{6,4},{8,10},{10,8},{12,14},{14,12},{16,18},{18,... | collective-permute-start | bytes 393224 | tf_op jit(solution)/shard_map/ppermute | solution.py:280
  25.8 4.0 %copy-start.2 = (bf16[1024]{0:T(1024)(128)(2,1)S(1)}, bf16[1024]{0:T(1024)(128)(2,1)}, u32[]{:S(2)}) copy-start(bf16[1024]{0:T(1024)(128)(2,1)} %param.11) | copy-start | bytes 6148
  25.9 4.7 %collective-permute-start.7 = (f32[128,128]{1,0:T(8,128)S(1)}, f32[128,128]{1,0:T(8,128)S(1)}, u32[]{:S(2)}, u32[]{:S(2)}) collective-permute-start(f32[128,128]{1,0:T(8,128)S(1)} %shard_map.69.refs_2_), channel_id=1, source_target_pairs={{0,1},{1,0},{2,3},{3,2},{4,5},{5,4},{6,7},{7,6},{8,9},{9,8},{10,11... | collective-permute-start | bytes 196616 | tf_op jit(solution)/shard_map/ppermute | solution.py:319

commit v3 on v2

--- a/solution.py
+++ b/solution.py
@@ -33,15 +33,21 @@
     return lax.rem(lax.axis_index("seq"), TEAM)
 
 
-def cut_halves(arrays, stay=True):
+def cut_halves(arrays, lengths=None):
     tokens, channels = arrays[0].shape
     share = channels // TEAM
     count = len(arrays)
+    first_cut = lengths is not None
 
     def body(*refs):
-        ins, outs = refs[:count], refs[count : count + TEAM]
-        held, sems = refs[count + TEAM :]
-        me = place()
+        ins, refs = refs[:count], refs[count:]
+        me = place()
+        if first_cut:
+            lengths_ref, *outs, starts_ref, held, sems, row_ref, row_sem = refs
+            row_copy = pltpu.make_async_copy(lengths_ref, row_ref, row_sem)
+            row_copy.start()
+        else:
+            *outs, held, sems = refs
         copies = []
         for step in (1, 0):
             first = pl.multiple_of(lax.bitwise_xor(me, step) * share, share)
@@ -51,6 +57,10 @@
                 )
                 copy.start()
                 copies.append((copy, i, step))
+        if first_cut:
+            row_copy.wait()
+            base = (lax.axis_index("seq") - me) * tokens
+            starts_ref[...] = document_starts(row_ref[...], base, tokens)
         for copy, i, step in copies:
             copy.wait()
             outs[step][i * share : (i + 1) * share, :] = held[i, step].T
@@ -60,9 +70,13 @@
         VMEM((count, TEAM, tokens, share), BF16),
         pltpu.SemaphoreType.DMA((count, TEAM)),
     ]
-    if stay:
-        arrays = [pltpu.with_memory_space_constraint(a, pltpu.HBM) for a in arrays]
-    return kernel_call(body, outs, arrays, scratch, spaces=[pl.ANY] * count)
+    args = list(arrays)
+    if first_cut:
+        row = lengths.reshape(1, lengths.shape[0])
+        args = [pltpu.with_memory_space_constraint(a, pltpu.HBM) for a in args + [row]]
+        outs.append(jax.ShapeDtypeStruct((TEAM, tokens), jnp.int32))
+        scratch += [VMEM(row.shape, jnp.int32), pltpu.SemaphoreType.DMA]
+    return kernel_call(body, outs, args, scratch, spaces=[pl.ANY] * len(args))
 
 
 def bands(row):
@@ -96,8 +110,41 @@
     return (mixed / totals).astype(BF16)
 
 
+def document_starts(lengths, base, tokens):
+    docs = lengths.shape[1]
+    until = lax.broadcasted_iota(jnp.int32, (docs, docs), 1) <= lax.broadcasted_iota(
+        jnp.int32, (docs, docs), 0
+    )
+    spread = jnp.broadcast_to(lengths.astype(F32), (docs, docs))
+    ends = jnp.sum(jnp.where(until, spread, 0.0), axis=1, keepdims=True)
+    rows = []
+    for block in range(TEAM):
+        first = base + block * tokens
+        pos = (lax.broadcasted_iota(jnp.int32, (docs, tokens), 1) + first).astype(F32)
+        begun = jnp.max(jnp.where(ends <= pos, ends, 0.0), axis=0, keepdims=True)
+        rows.append(begun.astype(jnp.int32) - first)
+    return jnp.concatenate(rows, 0)
+
+
 def gated(x_now, conv):
     return (x_now.astype(F32) * conv).astype(BF16)
+
+
+def second_queries(q_own, q_got, after):
+    def body(own_ref, got_ref, after_ref, out_ref):
+        me = place()
+
+        @pl.when(me == 0)
+        def _():
+            out_ref[...] = got_ref[...]
+
+        @pl.when(me != 0)
+        def _():
+            out_ref[...] = own_ref[...]
+
+    outs = [jax.ShapeDtypeStruct(q_own.shape, BF16)]
+    flops = 2 * 3 * q_own.size * 256 * 8
+    return kernel_call(body, outs, [q_own, q_got, after], (), flops, [VMEM, VMEM, pl.ANY])[0]
 
 
 def second_conv(q_own, q_got, kv_own, kv_got, filters):
@@ -105,7 +152,7 @@
     team_groups = filters.shape[1] // TEAM
     width = share // team_groups
 
-    def body(q_own_ref, q_got_ref, kv_own_ref, kv_got_ref, filter_ref, raw_ref, last_ref, q1_ref, k1_ref, v1_ref, x_ref, y_ref):
+    def body(q_own_ref, q_got_ref, kv_own_ref, kv_got_ref, filter_ref, raw_ref, q1_ref, k1_ref, v1_ref, x_ref, y_ref):
         me = place()
         other = 1 - me
         x_ref[me, 0] = q_own_ref[...]
@@ -115,7 +162,6 @@
         x_ref[other, 1] = kv_got_ref[:share]
         x_ref[other, 2] = kv_got_ref[share:]
         raw_ref[...] = x_ref[0]
-        last_ref[...] = x_ref[1, 0]
         for part in range(3):
             rows = filter_rows(filter_ref, part, me)
             for group in range(team_groups):
@@ -133,7 +179,6 @@
     outs = [
         sds((3, share, tokens), BF16),
         sds((share, tokens), BF16),
-        sds((share, tokens), BF16),
         sds((tokens, share), BF16),
         sds((share, tokens), BF16),
     ]
@@ -142,12 +187,17 @@
     return kernel_call(body, outs, [q_own, q_got, kv_own, kv_got, filters], scratch, flops)
 
 
+def square_row(head_out):
+    wide = head_out.astype(F32)
+    return jnp.sum(wide * wide, axis=0, keepdims=True)
+
+
 def rim_keys(rim_own, rim_got, raw, q1, k1, v1, filters, starts):
     share, tokens = q1.shape
     team_groups = filters.shape[1] // TEAM
     width = share // team_groups
 
-    def body(own_ref, got_ref, raw_ref, q1_ref, k1_ref, v1_ref, filter_ref, starts_ref, k_ref, v_ref, out_ref, rim_ref, y_ref):
+    def body(own_ref, got_ref, raw_ref, q1_ref, k1_ref, v1_ref, filter_ref, starts_ref, k_ref, v_ref, out_ref, sum_ref, rim_ref, y_ref):
         me = place()
         rim_ref[me] = own_ref[...]
         rim_ref[1 - me] = got_ref[...]
@@ -171,6 +221,7 @@
                 else:
                     v_ref[at, :tokens] = far
                     v_ref[at, tokens:] = near
+        total = jnp.zeros((1, tokens), F32)
         for first in range(0, share, HDIM):
             at = slice(first, first + HDIM)
             k_ref[:tokens, at] = y_ref[at, :tokens].T
@@ -183,24 +234,27 @@
                 starts_ref[1:2, :],
             )
             out_ref[:, at] = out.T
+            total = total + square_row(out)
+        sum_ref[...] = jnp.broadcast_to(total, (8, tokens))
 
     sds = jax.ShapeDtypeStruct
     outs = [
         sds((2 * tokens, share), BF16),
         sds((share, 2 * tokens), BF16),
         sds((tokens, share), BF16),
+        sds((8, tokens), F32),
     ]
     scratch = [VMEM((TEAM, 2 * share, tokens), BF16), VMEM((share, 2 * tokens), BF16)]
     args = [rim_own, rim_got, raw, q1, k1, v1, filters, starts]
     return kernel_call(body, outs, args, scratch, 2 * 2 * share * tokens * 2 * tokens * 8)
 
 
-def first_attention(rim_q, raw, keys, values, second, filters, starts):
+def first_attention(rim_q, raw, keys, values, second, second_sum, filters, starts):
     share, tokens = rim_q.shape
     team_groups = filters.shape[1] // TEAM
     width = share // team_groups
 
-    def body(rim_ref, raw_ref, k_ref, v_ref, second_ref, filter_ref, starts_ref, keep_ref, send_ref, y_ref, out_ref):
+    def body(rim_ref, raw_ref, k_ref, v_ref, second_ref, second_sum_ref, filter_ref, starts_ref, keep_ref, send_ref, sum_ref, y_ref, out_ref):
         me = place()
         rows = filter_rows(filter_ref, 0, me)
         for group in range(team_groups):
@@ -209,34 +263,26 @@
             left = jnp.concatenate([rim_ref[at], now], 1)
             conv = jnp.dot(left, bands(rows[group : group + 1]), preferred_element_type=F32)
             y_ref[at] = gated(now, conv)
+        total = jnp.zeros((1, tokens), F32)
         for first in range(0, share, HDIM):
             at = slice(first, first + HDIM)
             out = attend_head(y_ref[at], k_ref[:, at], v_ref[at, :], starts_ref[0:1, :])
             out_ref[0, :, at] = out.T
+            total = total + square_row(out)
         out_ref[1] = second_ref[...]
+        row = lax.broadcasted_iota(jnp.int32, (8, tokens), 0)
+        sum_ref[...] = jnp.where(row == 0, jnp.broadcast_to(total, (8, tokens)), second_sum_ref[...])
         keep_ref[...] = out_ref[me]
         send_ref[...] = out_ref[1 - me]
 
     outs = [jax.ShapeDtypeStruct((tokens, share), BF16)] * 2
+    outs += [jax.ShapeDtypeStruct((8, tokens), F32)]
     scratch = [VMEM((share, tokens), BF16), VMEM((TEAM, tokens, share), BF16)]
-    args = [rim_q, raw, keys, values, second, filters, starts]
+    args = [rim_q, raw, keys, values, second, second_sum, filters, starts]
     return kernel_call(body, outs, args, scratch, 2 * share * tokens * 2 * tokens * 8)
 
 
-def square_sums(parts):
-    tokens = parts[0].shape[0]
-
-    def body(*refs):
-        total = jnp.zeros((tokens, 1), F32)
-        for ref in refs[:-1]:
-            wide = ref[...].astype(F32)
-            total = total + jnp.sum(wide * wide, axis=1, keepdims=True)
-        refs[-1][...] = jnp.broadcast_to(total, (tokens, 128))
-
-    return kernel_call(body, [jax.ShapeDtypeStruct((tokens, 128), F32)], parts)[0]
-
-
-def scaled(parts, sums, gain, total_channels):
+def scaled(parts, sums, gain, total_channels, count_got):
     tokens, share = parts[0].shape
     count = len(sums)
 
@@ -244,9 +290,13 @@
         part_refs, sum_refs = refs[:TEAM], refs[TEAM : TEAM + count]
         gain_ref, out_ref, held, sems = refs[TEAM + count :]
         me = place()
-        total = sum_refs[0][...]
-        for ref in sum_refs[1:]:
-            total = total + ref[...]
+        total = jnp.zeros((1, tokens), F32)
+        for ref in sum_refs:
+            total = total + ref[pl.ds(me, 1), :]
+        total = jnp.broadcast_to(total, (128, tokens)).T
+        if count_got:
+            wide = part_refs[1][...].astype(F32)
+            total = total + jnp.sum(wide * wide, axis=1, keepdims=True)
         scale = lax.rsqrt(total / total_channels + 1e-06)
         piece = share // 2
         scale = jnp.concatenate([scale] * (piece // 128), 1)
@@ -285,41 +335,36 @@
     return lax.ppermute(value, "seq", [(i, i + TEAM) for i in range(count - TEAM)])
 
 
-def document_starts(lengths, tokens):
-    ends = jnp.cumsum(lengths)
-    base = (lax.axis_index("seq") // TEAM) * (TEAM * tokens)
-    pos = base + jnp.arange(TEAM * tokens, dtype=jnp.int32)
-    begun = jnp.where(ends[:, None] <= pos[None, :], ends[:, None], 0)
-    first = jnp.max(begun, axis=0).reshape(TEAM, tokens)
-    block_base = base + tokens * jnp.arange(TEAM, dtype=jnp.int32)
-    return first - block_base[:, None]
-
-
 def per_device(q_in, k_in, v_in, filters, lengths, gain):
     tokens, channels = q_in.shape
-    kv_own, kv_other = cut_halves([k_in, v_in])
+    kv_own, kv_other, starts = cut_halves([k_in, v_in], lengths)
     half = kv_other.shape[0] // 2
     k_got = swapped(kv_other[:half])
     v_got = swapped(kv_other[half:])
-    q_own, q_other = cut_halves([q_in], stay=False)
+    q_own, q_other = cut_halves([q_in])
     q_other, k_got = lax.optimization_barrier((q_other, k_got))
     q_got = swapped(q_other)
     rim_own = onward(kv_own)
     kv_got = jnp.concatenate([k_got, v_got], 0)
     rim_got = onward(kv_got)
-    starts = document_starts(lengths, tokens)
-    raw, last_q, q1, k1, v1 = second_conv(q_own, q_got, kv_own, kv_got, filters)
-    rim_q = onward(last_q)
-    keys, values, second = rim_keys(rim_own, rim_got, raw, q1, k1, v1, filters, starts)
-    keep, send = first_attention(rim_q, raw, keys, values, second, filters, starts)
+    rim_q = onward(second_queries(q_own, q_got, kv_got))
+    raw, q1, k1, v1 = second_conv(q_own, q_got, kv_own, kv_got, filters)
+    keys, values, second, second_sum = rim_keys(rim_own, rim_got, raw, q1, k1, v1, filters, starts)
+    keep, send, own = first_attention(
+        rim_q, raw, keys, values, second, second_sum, filters, starts
+    )
     mine = [keep, swapped(send)]
-    own = square_sums(mine)
     head_count = lax.axis_size("head")
     if head_count == 2:
-        sums = [own, lax.ppermute(own, "head", [(0, 1), (1, 0)])]
-    else:
-        sums = [lax.psum(own, "head")]
-    return scaled(mine, sums, gain, channels * head_count)
+        cross = [(i, i ^ 3) for i in range(2 * lax.axis_size("seq"))]
+        sums = [
+            own,
+            lax.ppermute(own, "head", [(0, 1), (1, 0)]),
+            lax.ppermute(own, ("seq", "head"), cross),
+        ]
+        return scaled(mine, sums, gain, channels * head_count, True)
+    own = lax.psum(own, "head")
+    return scaled(mine, [own, swapped(own)], gain, channels * head_count, False)
 
 
 def solution(mesh):

time: 31.7 us -> 29.7 us (0.937)
  the two profiles are of different devices: /device:TPU:27 before, /device:TPU:9 now
where the time goes in v3:
time: 29.7 us; the launch traced here: 29.5 us
  starting transfers between devices  16.8 us (57%)
  waiting for transfers between devices  6.76 us (23%)
  Pallas kernels  5.72 us (19%)
    ppermute x3, starting transfers between devices, onward(): lax.ppermute(value, 'seq', [(i, i + TEAM) for i in range(count - TEAM)])  9.43 us
    pallas_call x7, Pallas kernels, kernel_call(): pl.pallas_call(body, out_shape=outs, in_specs=[pl.BlockSpec(memory_space=...  5.72 us
    ppermute x4, starting transfers between devices, swapped(): return lax.ppermute(value, 'seq', [(i, i ^ 1) for i in range(count)])  4.08 us
    ppermute x1, starting transfers between devices, per_device(): lax.ppermute(own, 'head', [(0, 1), (1, 0)])  3.14 us
    ppermute x3, waiting for transfers between devices, onward(): lax.ppermute(value, 'seq', [(i, i + TEAM) for i in range(count - TEAM)])  2.78 us
    ppermute x1, waiting for transfers between devices, per_device(): lax.ppermute(own, ('seq', 'head'), cross)  2.3 us
    ppermute x4, waiting for transfers between devices, swapped(): return lax.ppermute(value, 'seq', [(i, i ^ 1) for i in range(count)])  1 us
    ppermute x1, waiting for transfers between devices, per_device(): lax.ppermute(own, 'head', [(0, 1), (1, 0)])  0.67 us
  transfers between devices with their start and end apart: 9, of which 5 were waited for; matrix products, arithmetic and copies ran while one was open for 0% of the time, Pallas kernels for 9%

profile of v3, /device:TPU:9, one launch (start us, length us, event | category | flops | bytes accessed | tf_op | source)
XLA Modules:
  0.0 29.5 jit_solution(8629527085606216410)
XLA Ops:
  0.0 1.3 %shard_map.65 = (bf16[1024,128]{1,0:T(8,128)(2,1)S(1)}, bf16[1024,128]{1,0:T(8,128)(2,1)S(1)}, s32[2,128]{1,0:T(2,128)S(1)}) custom-call(bf16[128,1024]{1,0:T(8,128)(2,1)} %refs_0_.3, bf16[128,1024]{1,0:T(8,128)(2,1)} %refs_1_.1, s32[1,32]{1,0:T(1,128)} %bitcast.1), custom_call_target="tpu_custom_call" | custom-call | bytes 1049728 | tf_op jit(solution)/shard_map/pallas_call | solution.py:21
  1.3 0.0 copy-start
  1.4 1.3 %collective-permute-start = (bf16[512,128]{1,0:T(8,128)(2,1)S(1)}, bf16[512,128]{1,0:T(8,128)(2,1)S(1)}, u32[]{:S(2)}, u32[]{:S(2)}) collective-permute-start(bf16[512,128]{1,0:T(8,128)(2,1)S(1)} %get-tuple-element.42), channel_id=1, source_target_pairs={{0,2},{2,0},{4,6},{6,4},{8,10},{10,8},{12,14},{14,12},{16,18},{18,... | collective-permute-start | bytes 393224 | tf_op jit(solution)/shard_map/ppermute | solution.py:330
  2.6 0.3 collective-permute-start.2
  2.9 3.1 %collective-permute-start.4 = (bf16[1024,128]{1,0:T(8,128)(2,1)S(1)}, bf16[1024,128]{1,0:T(8,128)(2,1)S(1)}, u32[]{:S(2)}, u32[]{:S(2)}) collective-permute-start(bf16[1024,128]{1,0:T(8,128)(2,1)S(1)} %get-tuple-element.28.kv_own_ref), channel_id=1, source_target_pairs={{0,4},{2,6},{4,8},{6,10},{8,12},{10,14},{12,16},{14,18},{16,20},{1... | collective-permute-start | bytes 786440 | tf_op jit(solution)/shard_map/ppermute | solution.py:335
  6.1 0.3 shard_map.64
  6.3 1.3 %collective-permute-start.1 = (bf16[512,128]{1,0:T(8,128)(2,1)S(1)}, bf16[512,128]{1,0:T(8,128)(2,1)S(1)}, u32[]{:S(2)}, u32[]{:S(2)}) collective-permute-start(bf16[512,128]{1,0:T(8,128)(2,1)S(1)} %get-tuple-element.26), channel_id=1, source_target_pairs={{0,2},{2,0},{4,6},{6,4},{8,10},{10,8},{12,14},{14,12},{16,18},{18,... | collective-permute-start | bytes 393224 | tf_op jit(solution)/shard_map/ppermute | solution.py:330
  7.6 1.0 %collective-permute-done.2 = bf16[512,128]{1,0:T(8,128)(2,1)S(1)} collective-permute-done((bf16[512,128]{1,0:T(8,128)(2,1)S(1)}, bf16[512,128]{1,0:T(8,128)(2,1)S(1)}, u32[]{:S(2)}, u32[]{:S(2)}) %collective-permute-start.2) | collective-permute-done | bytes 131104 | tf_op jit(solution)/shard_map/ppermute | solution.py:330
  8.6 3.1 %collective-permute-start.5 = (bf16[1024,128]{1,0:T(8,128)(2,1)S(1)}, bf16[1024,128]{1,0:T(8,128)(2,1)S(1)}, u32[]{:S(2)}, u32[]{:S(2)}) collective-permute-start(bf16[1024,128]{1,0:T(8,128)(2,1)S(1)} %constant_dynamic-update-slice_fusion.after_ref.kv_got_ref), channel_id=1, source_target_pairs={{0,4},{2,6},{4,8},{6,10},{8,12},{10,14},{12,16},{14,18},{16,20},{1... | collective-permute-start | bytes 786440 | tf_op jit(solution)/shard_map/ppermute | solution.py:335
  11.8 0.0 copy-start.1
  11.8 3.1 %collective-permute-start.3 = (bf16[512,128]{1,0:T(8,128)(2,1)S(1)}, bf16[512,128]{1,0:T(8,128)(2,1)S(1)}, u32[]{:S(2)}, u32[]{:S(2)}) collective-permute-start(bf16[512,128]{1,0:T(8,128)(2,1)S(1)} %shard_map.66), channel_id=1, source_target_pairs={{0,4},{2,6},{4,8},{6,10},{8,12},{10,14},{12,16},{14,18},{16,20},{1... | collective-permute-start | bytes 393224 | tf_op jit(solution)/shard_map/ppermute | solution.py:335
  15.0 1.1 %shard_map.67 = (bf16[3,512,128]{2,1,0:T(8,128)(2,1)S(1)}, bf16[512,128]{1,0:T(8,128)(2,1)S(1)}, bf16[128,512]{1,0:T(8,128)(2,1)S(1)}, bf16[512,128]{1,0:T(8,128)(2,1)S(1)}) custom-call(bf16[512,128]{1,0:T(8,128)(2,1)S(1)} %get-tuple-element.23.own_ref.q_own_ref, bf16[512,128]{1,0:T(8,128)(2,1)S(1)} %collective-permute-done.1.got_ref.q_got_ref, ...), custom_call_target="tpu_custom_call" | custom-call | flops 805306368 | bytes 1622016 | tf_op jit(solution)/shard_map/pallas_call | solution.py:21
  16.1 0.0 collective-permute-done.4.own_ref
  16.1 1.0 %collective-permute-done.5.got_ref = bf16[1024,128]{1,0:T(8,128)(2,1)S(1)} collective-permute-done((bf16[1024,128]{1,0:T(8,128)(2,1)S(1)}, bf16[1024,128]{1,0:T(8,128)(2,1)S(1)}, u32[]{:S(2)}, u32[]{:S(2)}) %collective-permute-start.5) | collective-permute-done | bytes 262176 | tf_op jit(solution)/shard_map/ppermute | solution.py:335
  17.1 1.2 %shard_map.68 = (bf16[256,512]{1,0:T(8,128)(2,1)S(1)}, bf16[512,256]{1,0:T(8,128)(2,1)S(1)}, bf16[128,512]{1,0:T(8,128)(2,1)S(1)}, f32[8,128]{1,0:T(8,128)S(1)}) custom-call(bf16[1024,128]{1,0:T(8,128)(2,1)S(1)} %collective-permute-done.4.own_ref, bf16[1024,128]{1,0:T(8,128)(2,1)S(1)} %collective-permute-done.5.got_ref, ...), custom_call_target="tpu_custom_call" | custom-call | flops 536870912 | bytes 2020352 | tf_op jit(solution)/shard_map/pallas_call | solution.py:21
  18.3 1.8 %collective-permute-done.3.rim_ref = bf16[512,128]{1,0:T(8,128)(2,1)S(1)} collective-permute-done((bf16[512,128]{1,0:T(8,128)(2,1)S(1)}, bf16[512,128]{1,0:T(8,128)(2,1)S(1)}, u32[]{:S(2)}, u32[]{:S(2)}) %collective-permute-start.3) | collective-permute-done | bytes 131104 | tf_op jit(solution)/shard_map/ppermute | solution.py:335
  20.1 0.9 %shard_map.69 = (bf16[128,512]{1,0:T(8,128)(2,1)S(1)}, bf16[128,512]{1,0:T(8,128)(2,1)S(1)}, f32[8,128]{1,0:T(8,128)S(1)}) custom-call(bf16[512,128]{1,0:T(8,128)(2,1)S(1)} %collective-permute-done.3.rim_ref, bf16[3,512,128]{2,1,0:T(8,128)(2,1)S(1)} %get-tuple-element.29.raw_ref, bf16[256,512]{1,0:T(8,128)(2,1)S(1)} %get-tuple-element.34.k_ref, ...), custom_call_target="tpu_custom_call" | custom-call | flops 268435456 | bytes 1500160 | tf_op jit(solution)/shard_map/pallas_call | solution.py:21
  21.0 0.0 copy-start.2
  21.0 1.3 %collective-permute-start.6 = (bf16[128,512]{1,0:T(8,128)(2,1)S(1)}, bf16[128,512]{1,0:T(8,128)(2,1)S(1)}, u32[]{:S(2)}, u32[]{:S(2)}) collective-permute-start(bf16[128,512]{1,0:T(8,128)(2,1)S(1)} %get-tuple-element.39), channel_id=1, source_target_pairs={{0,2},{2,0},{4,6},{6,4},{8,10},{10,8},{12,14},{14,12},{16,18},{18,... | collective-permute-start | bytes 393224 | tf_op jit(solution)/shard_map/ppermute | solution.py:330
  22.3 3.1 %collective-permute-start.7 = (f32[8,128]{1,0:T(8,128)S(1)}, f32[8,128]{1,0:T(8,128)S(1)}, u32[]{:S(2)}, u32[]{:S(2)}) collective-permute-start(f32[8,128]{1,0:T(8,128)S(1)} %get-tuple-element.40.refs_2_), channel_id=1, source_target_pairs={{0,1},{1,0},{2,3},{3,2},{4,5},{5,4},{6,7},{7,6},{8,9},{9,8},{10,11... | collective-permute-start | bytes 12296 | tf_op jit(solution)/shard_map/ppermute | solution.py:362
  25.5 0.1 collective-permute-start.8
  25.6 0.7 %collective-permute-done.7.refs_3_ = f32[8,128]{1,0:T(8,128)S(1)} collective-permute-done((f32[8,128]{1,0:T(8,128)S(1)}, f32[8,128]{1,0:T(8,128)S(1)}, u32[]{:S(2)}, u32[]{:S(2)}) %collective-permute-start.7) | collective-permute-done | bytes 4128 | tf_op jit(solution)/shard_map/ppermute | solution.py:362
  26.3 2.3 %collective-permute-done.8.refs_4_ = f32[8,128]{1,0:T(8,128)S(1)} collective-permute-done((f32[8,128]{1,0:T(8,128)S(1)}, f32[8,128]{1,0:T(8,128)S(1)}, u32[]{:S(2)}, u32[]{:S(2)}) %collective-permute-start.8) | collective-permute-done | bytes 4128 | tf_op jit(solution)/shard_map/ppermute | solution.py:363
  28.6 0.9 %shard_map.70 = bf16[128,1024]{1,0:T(8,128)(2,1)} custom-call(bf16[128,512]{1,0:T(8,128)(2,1)S(1)} %get-tuple-element.38.refs_0_, bf16[128,512]{1,0:T(8,128)(2,1)S(1)} %collective-permute-done.6.refs_1_, f32[8,128]{1,0:T(8,128)S(1)} %get-tuple-element.40.refs_2_, f32[8,128]{1,0:T(8,128)S(1)} %collective-permute-done.7.refs_3_, ...), custom_call_target="tpu_custom_call" | custom-call | bytes 538624 | tf_op jit(solution)/shard_map/pallas_call | solution.py:21
  (11 shorter events, 0.1 us)
Async XLA Ops:
  1.3 4.7 %copy-start = (bf16[128,1024]{1,0:T(8,128)(2,1)S(1)}, bf16[128,1024]{1,0:T(8,128)(2,1)}, u32[]{:S(2)}) copy-start(bf16[128,1024]{1,0:T(8,128)(2,1)} %refs_0_.2) | copy-start | bytes 786436
  1.4 4.9 %collective-permute-start = (bf16[512,128]{1,0:T(8,128)(2,1)S(1)}, bf16[512,128]{1,0:T(8,128)(2,1)S(1)}, u32[]{:S(2)}, u32[]{:S(2)}) collective-permute-start(bf16[512,128]{1,0:T(8,128)(2,1)S(1)} %get-tuple-element.42), channel_id=1, source_target_pairs={{0,2},{2,0},{4,6},{6,4},{8,10},{10,8},{12,14},{14,12},{16,18},{18,... | collective-permute-start | bytes 393224 | tf_op jit(solution)/shard_map/ppermute | solution.py:330
  2.6 6.0 %collective-permute-start.2 = (bf16[512,128]{1,0:T(8,128)(2,1)S(1)}, bf16[512,128]{1,0:T(8,128)(2,1)S(1)}, u32[]{:S(2)}, u32[]{:S(2)}) collective-permute-start(bf16[512,128]{1,0:T(8,128)(2,1)S(1)} %get-tuple-element.41), channel_id=1, source_target_pairs={{0,2},{2,0},{4,6},{6,4},{8,10},{10,8},{12,14},{14,12},{16,18},{18,... | collective-permute-start | bytes 393224 | tf_op jit(solution)/shard_map/ppermute | solution.py:330
  2.9 13.2 %collective-permute-start.4 = (bf16[1024,128]{1,0:T(8,128)(2,1)S(1)}, bf16[1024,128]{1,0:T(8,128)(2,1)S(1)}, u32[]{:S(2)}, u32[]{:S(2)}) collective-permute-start(bf16[1024,128]{1,0:T(8,128)(2,1)S(1)} %get-tuple-element.28.kv_own_ref), channel_id=1, source_target_pairs={{0,4},{2,6},{4,8},{6,10},{8,12},{10,14},{12,16},{14,18},{16,20},{1... | collective-permute-start | bytes 786440 | tf_op jit(solution)/shard_map/ppermute | solution.py:335
  6.3 5.5 %collective-permute-start.1 = (bf16[512,128]{1,0:T(8,128)(2,1)S(1)}, bf16[512,128]{1,0:T(8,128)(2,1)S(1)}, u32[]{:S(2)}, u32[]{:S(2)}) collective-permute-start(bf16[512,128]{1,0:T(8,128)(2,1)S(1)} %get-tuple-element.26), channel_id=1, source_target_pairs={{0,2},{2,0},{4,6},{6,4},{8,10},{10,8},{12,14},{14,12},{16,18},{18,... | collective-permute-start | bytes 393224 | tf_op jit(solution)/shard_map/ppermute | solution.py:330
  8.6 8.5 %collective-permute-start.5 = (bf16[1024,128]{1,0:T(8,128)(2,1)S(1)}, bf16[1024,128]{1,0:T(8,128)(2,1)S(1)}, u32[]{:S(2)}, u32[]{:S(2)}) collective-permute-start(bf16[1024,128]{1,0:T(8,128)(2,1)S(1)} %constant_dynamic-update-slice_fusion.after_ref.kv_got_ref), channel_id=1, source_target_pairs={{0,4},{2,6},{4,8},{6,10},{8,12},{10,14},{12,16},{14,18},{16,20},{1... | collective-permute-start | bytes 786440 | tf_op jit(solution)/shard_map/ppermute | solution.py:335
  11.8 3.2 %copy-start.1 = (bf16[3,64,128]{2,1,0:T(8,128)(2,1)S(1)}, bf16[3,64,128]{2,1,0:T(8,128)(2,1)}, u32[]{:S(2)}) copy-start(bf16[3,64,128]{2,1,0:T(8,128)(2,1)} %filter_ref.5) | copy-start | bytes 147460
  11.8 8.2 %collective-permute-start.3 = (bf16[512,128]{1,0:T(8,128)(2,1)S(1)}, bf16[512,128]{1,0:T(8,128)(2,1)S(1)}, u32[]{:S(2)}, u32[]{:S(2)}) collective-permute-start(bf16[512,128]{1,0:T(8,128)(2,1)S(1)} %shard_map.66), channel_id=1, source_target_pairs={{0,4},{2,6},{4,8},{6,10},{8,12},{10,14},{12,16},{14,18},{16,20},{1... | collective-permute-start | bytes 393224 | tf_op jit(solution)/shard_map/ppermute | solution.py:335
  21.0 4.6 %copy-start.2 = (bf16[1024]{0:T(1024)(128)(2,1)S(1)}, bf16[1024]{0:T(1024)(128)(2,1)}, u32[]{:S(2)}) copy-start(bf16[1024]{0:T(1024)(128)(2,1)} %param.11) | copy-start | bytes 6148
  21.0 7.5 %collective-permute-start.6 = (bf16[128,512]{1,0:T(8,128)(2,1)S(1)}, bf16[128,512]{1,0:T(8,128)(2,1)S(1)}, u32[]{:S(2)}, u32[]{:S(2)}) collective-permute-start(bf16[128,512]{1,0:T(8,128)(2,1)S(1)} %get-tuple-element.39), channel_id=1, source_target_pairs={{0,2},{2,0},{4,6},{6,4},{8,10},{10,8},{12,14},{14,12},{16,18},{18,... | collective-permute-start | bytes 393224 | tf_op jit(solution)/shard_map/ppermute | solution.py:330
  22.3 4.0 %collective-permute-start.7 = (f32[8,128]{1,0:T(8,128)S(1)}, f32[8,128]{1,0:T(8,128)S(1)}, u32[]{:S(2)}, u32[]{:S(2)}) collective-permute-start(f32[8,128]{1,0:T(8,128)S(1)} %get-tuple-element.40.refs_2_), channel_id=1, source_target_pairs={{0,1},{1,0},{2,3},{3,2},{4,5},{5,4},{6,7},{7,6},{8,9},{9,8},{10,11... | collective-permute-start | bytes 12296 | tf_op jit(solution)/shard_map/ppermute | solution.py:362
  25.5 3.1 %collective-permute-start.8 = (f32[8,128]{1,0:T(8,128)S(1)}, f32[8,128]{1,0:T(8,128)S(1)}, u32[]{:S(2)}, u32[]{:S(2)}) collective-permute-start(f32[8,128]{1,0:T(8,128)S(1)} %get-tuple-element.40.refs_2_), channel_id=1, source_target_pairs={{0,3},{1,2},{2,1},{3,0},{4,7},{5,6},{6,5},{7,4},{8,11},{9,10},{10,... | collective-permute-start | bytes 12296 | tf_op jit(solution)/shard_map/ppermute | solution.py:363

commit v4 on v3

v4 whole, which is shorter than its diff:
```python
import math

import jax
import jax.numpy as jnp
from jax import lax
from jax.experimental import pallas as pl
from jax.experimental.pallas import tpu as pltpu
from jax.sharding import PartitionSpec as P

HDIM = 128
TEAM = 2
VMEM = pltpu.VMEM
F32 = jnp.float32
BF16 = jnp.bfloat16


def kernel_call(body, outs, args, scratch=(), flops=0, spaces=None, out_spaces=None):
    spaces = spaces or [VMEM] * len(args)
    out_spaces = out_spaces or [VMEM] * len(outs)
    moved = sum(math.prod(a.shape) * a.dtype.itemsize for a in list(args) + list(outs))
    return pl.pallas_call(
        body,
        out_shape=outs,
        in_specs=[pl.BlockSpec(memory_space=space) for space in spaces],
        out_specs=[pl.BlockSpec(memory_space=space) for space in out_spaces],
        scratch_shapes=list(scratch),
        compiler_params=pltpu.CompilerParams(vmem_limit_bytes=40 * 1024 * 1024),
        cost_estimate=pl.CostEstimate(flops=flops, bytes_accessed=moved, transcendentals=0),
    )(*args)


def place():
    return lax.rem(lax.axis_index("seq"), TEAM)


def cut_keys_values(k_in, v_in, lengths):
    tokens, channels = k_in.shape
    share = channels // TEAM
    row = lengths.reshape(1, lengths.shape[0])

    def body(k_ref, v_ref, row_hbm, own_ref, k_other_ref, v_other_ref, starts_ref, row_ref, sems):
        me = place()
        own = pl.ds(pl.multiple_of(me * share, share), share)
        other = pl.ds(pl.multiple_of((1 - me) * share, share), share)
        moves = [
            (k_ref.at[:, other], k_other_ref),
            (v_ref.at[:, other], v_other_ref),
            (row_hbm, row_ref),
            (k_ref.at[:, own], own_ref.at[0]),
            (v_ref.at[:, own], own_ref.at[1]),
        ]
        copies = [
            pltpu.make_async_copy(source, target, sems.at[i])
            for i, (source, target) in enumerate(moves)
        ]
        for copy in copies:
            copy.start()
        copies[2].wait()
        base = (lax.axis_index("seq") - me) * tokens
        starts_ref[...] = document_starts(row_ref[...], base, tokens)
        for i in (0, 1, 3, 4):
            copies[i].wait()

    sds = jax.ShapeDtypeStruct
    outs = [
        sds((2, tokens, share), BF16),
        sds((tokens, share), BF16),
        sds((tokens, share), BF16),
        sds((TEAM, tokens), jnp.int32),
    ]
    scratch = [VMEM(row.shape, jnp.int32), pltpu.SemaphoreType.DMA((5,))]
    args = [pltpu.with_memory_space_constraint(a, pltpu.HBM) for a in (k_in, v_in, row)]
    return kernel_call(body, outs, args, scratch, spaces=[pl.ANY] * 3)


def cut_queries(q_in):
    tokens, channels = q_in.shape
    share = channels // TEAM

    def body(ref, own_ref, other_ref):
        me = place()
        own_ref[...] = ref[:, pl.ds(pl.multiple_of(me * share, share), share)].T
        other_ref[...] = ref[:, pl.ds(pl.multiple_of((1 - me) * share, share), share)].T

    return kernel_call(body, [jax.ShapeDtypeStruct((share, tokens), BF16)] * 2, [q_in])


def bands(row):
    taps = row.shape[1]
    turned = pltpu.roll(jnp.broadcast_to(row, (taps, taps)), 0, 1, stride=1, stride_axis=0)
    lag = lax.broadcasted_iota(jnp.int32, (taps, taps), 1) - lax.broadcasted_iota(
        jnp.int32, (taps, taps), 0
    )
    zero = jnp.zeros_like(turned)
    earlier = jnp.where(lag < 0, turned, zero).astype(BF16)
    current = jnp.where(lag >= 0, turned, zero).astype(BF16)
    return jnp.concatenate([earlier, current], 0)


def filter_rows(filter_ref, part, me):
    team_groups = filter_ref.shape[1] // TEAM
    first = pl.multiple_of(me * team_groups, team_groups)
    return filter_ref[part, pl.ds(first, team_groups), :].astype(F32)


def attend_heads(q_cols, k_rows, v_cols, starts):
    span, tokens = k_rows[0].shape[0], q_cols[0].shape[1]
    key_pos = lax.broadcasted_iota(jnp.int32, (span, tokens), 0) - tokens
    query_pos = lax.broadcasted_iota(jnp.int32, (span, tokens), 1)
    allowed = (key_pos >= starts) & (key_pos <= query_pos)
    scores = [jnp.dot(k, q, preferred_element_type=F32) for k, q in zip(k_rows, q_cols)]
    scores = [jnp.where(allowed, s * (1.0 / math.sqrt(HDIM)), -1e30) for s in scores]
    weights = [jnp.exp(s - jnp.max(s, axis=0, keepdims=True)) for s in scores]
    totals = [jnp.sum(w, axis=0, keepdims=True) for w in weights]
    mixed = [
        jnp.dot(v, w.astype(BF16), preferred_element_type=F32) for v, w in zip(v_cols, weights)
    ]
    return [(m / t).astype(BF16) for m, t in zip(mixed, totals)]


def document_starts(lengths, base, tokens):
    docs = lengths.shape[1]
    until = lax.broadcasted_iota(jnp.int32, (docs, docs), 1) <= lax.broadcasted_iota(
        jnp.int32, (docs, docs), 0
    )
    spread = jnp.broadcast_to(lengths.astype(F32), (docs, docs))
    ends = jnp.sum(jnp.where(until, spread, 0.0), axis=1, keepdims=True)
    rows = []
    for block in range(TEAM):
        first = base + block * tokens
        pos = (lax.broadcasted_iota(jnp.int32, (docs, tokens), 1) + first).astype(F32)
        begun = jnp.max(jnp.where(ends <= pos, ends, 0.0), axis=0, keepdims=True)
        rows.append(begun.astype(jnp.int32) - first)
    return jnp.concatenate(rows, 0)


def gated(x_now, conv):
    return (x_now.astype(F32) * conv).astype(BF16)


def second_queries(q_own, q_got, after):
    def body(own_ref, got_ref, after_ref, out_ref):
        me = place()

        @pl.when(me == 0)
        def _():
            out_ref[...] = got_ref[...]

        @pl.when(me != 0)
        def _():
            out_ref[...] = own_ref[...]

    outs = [jax.ShapeDtypeStruct(q_own.shape, BF16)]
    flops = 2 * 3 * q_own.size * 256 * 8
    return kernel_call(body, outs, [q_own, q_got, after], (), flops, [VMEM, VMEM, pl.ANY])[0]


def second_conv(q_own, q_got, kv_own, kv_got, filters):
    share, tokens = q_own.shape
    team_groups = filters.shape[1] // TEAM
    width = share // team_groups

    def body(q_own_ref, q_got_ref, kv_own_ref, kv_got_ref, filter_ref, raw_ref, ear_ref, part_ref, q1_ref, k1_ref, v1_ref, x_ref, y_ref):
        me = place()
        other = 1 - me
        x_ref[me, 0] = q_own_ref[...]
        x_ref[me, 1] = kv_own_ref[0].T
        x_ref[me, 2] = kv_own_ref[1].T
        x_ref[other, 0] = q_got_ref[...]
        x_ref[other, 1] = kv_got_ref[0].T
        x_ref[other, 2] = kv_got_ref[1].T
        raw_ref[...] = x_ref[0]
        for part in range(3):
            rows = filter_rows(filter_ref, part, me)
            for group in range(team_groups):
                at = slice(group * width, (group + 1) * width)
                now = x_ref[1, part, at]
                before = x_ref[0, part, at]
                band = bands(rows[group : group + 1])
                left = jnp.concatenate([before, now], 1)
                if part == 0:
                    alone = jnp.concatenate([jnp.zeros_like(before), before], 1)
                    left = jnp.concatenate([left, alone], 0)
                    ear_ref[group * tokens : (group + 1) * tokens, :] = band[:tokens]
                conv = jnp.dot(left, band, preferred_element_type=F32)
                y_ref[part, at] = gated(now, conv[:width])
                if part == 0:
                    part_ref[at] = conv[width:]
        q1_ref[...] = y_ref[0]
        v1_ref[...] = y_ref[2]
        for first in range(0, share, HDIM):
            k1_ref[:, first : first + HDIM] = y_ref[1, first : first + HDIM].T

    sds = jax.ShapeDtypeStruct
    outs = [
        sds((3, share, tokens), BF16),
        sds((team_groups * tokens, tokens), BF16),
        sds((share, tokens), F32),
        sds((share, tokens), BF16),
        sds((tokens, share), BF16),
        sds((share, tokens), BF16),
    ]
    scratch = [VMEM((TEAM, 3, share, tokens), BF16), VMEM((3, share, tokens), BF16)]
    flops = 2 * 3 * share * tokens * 2 * tokens * 8
    return kernel_call(body, outs, [q_own, q_got, kv_own, kv_got, filters], scratch, flops)


def square_row(head_out):
    wide = head_out.astype(F32)
    return jnp.sum(wide * wide, axis=0, keepdims=True)


def rim_keys(rim_own, rim_got, raw, q1, k1, v1, filters, starts):
    share, tokens = q1.shape
    team_groups = filters.shape[1] // TEAM
    width = share // team_groups

    def body(own_ref, got_ref, raw_ref, q1_ref, k1_ref, v1_ref, filter_ref, starts_ref, k_ref, v_ref, out_ref, sum_ref, rim_ref, y_ref):
        me = place()
        for part in range(2):
            rim_ref[me, part * share : (part + 1) * share] = own_ref[part].T
            rim_ref[1 - me, part * share : (part + 1) * share] = got_ref[part].T
        for part in (1, 2):
            rows = filter_rows(filter_ref, part, me)
            for group in range(team_groups):
                at = slice(group * width, (group + 1) * width)
                base = (part - 1) * share + group * width
                further = rim_ref[0, base : base + width]
                before = rim_ref[1, base : base + width]
                now = raw_ref[part, at]
                left = jnp.concatenate(
                    [jnp.concatenate([further, before], 1), jnp.concatenate([before, now], 1)], 0
                )
                conv = jnp.dot(left, bands(rows[group : group + 1]), preferred_element_type=F32)
                far = gated(before, conv[:width])
                near = gated(now, conv[width:])
                if part == 1:
                    y_ref[at, :tokens] = far
                    y_ref[at, tokens:] = near
                else:
                    v_ref[at, :tokens] = far
                    v_ref[at, tokens:] = near
        heads = [slice(first, first + HDIM) for first in range(0, share, HDIM)]
        k_rows = []
        for at in heads:
            k_ref[:tokens, at] = y_ref[at, :tokens].T
            near = y_ref[at, tokens:].T
            k_ref[tokens:, at] = near
            k_rows.append(jnp.concatenate([near, k1_ref[:, at]], 0))
        outs = attend_heads(
            [q1_ref[at, :] for at in heads],
            k_rows,
            [jnp.concatenate([v_ref[at, tokens:], v1_ref[at, :]], 1) for at in heads],
            starts_ref[1:2, :],
        )
        total = jnp.zeros((1, tokens), F32)
        for at, out in zip(heads, outs):
            out_ref[:, at] = out.T
            total = total + square_row(out)
        sum_ref[...] = jnp.broadcast_to(total, (8, tokens))

    sds = jax.ShapeDtypeStruct
    outs = [
        sds((2 * tokens, share), BF16),
        sds((share, 2 * tokens), BF16),
        sds((tokens, share), BF16),
        sds((8, tokens), F32),
    ]
    scratch = [VMEM((TEAM, 2 * share, tokens), BF16), VMEM((share, 2 * tokens), BF16)]
    args = [rim_own, rim_got, raw, q1, k1, v1, filters, starts]
    return kernel_call(body, outs, args, scratch, 2 * 2 * share * tokens * 2 * tokens * 8)


def first_attention(rim_q, raw, ear, part, keys, values, second, second_sum, starts):
    share, tokens = rim_q.shape
    team_groups = ear.shape[0] // tokens
    width = share // team_groups

    def body(rim_ref, raw_ref, ear_ref, part_ref, k_ref, v_ref, second_ref, second_sum_ref, starts_ref, keep_ref, send_ref, sum_ref, y_ref, out_ref):
        me = place()
        for group in range(team_groups):
            at = slice(group * width, (group + 1) * width)
            band = ear_ref[group * tokens : (group + 1) * tokens, :]
            conv = part_ref[at] + jnp.dot(rim_ref[at], band, preferred_element_type=F32)
            y_ref[at] = gated(raw_ref[0, at], conv)
        heads = [slice(first, first + HDIM) for first in range(0, share, HDIM)]
        outs = attend_heads(
            [y_ref[at] for at in heads],
            [k_ref[:, at] for at in heads],
            [v_ref[at, :] for at in heads],
            starts_ref[0:1, :],
        )
        total = jnp.zeros((1, tokens), F32)
        for at, out in zip(heads, outs):
            out_ref[0, :, at] = out.T
            total = total + square_row(out)
        out_ref[1] = second_ref[...]
        row = lax.broadcasted_iota(jnp.int32, (8, tokens), 0)
        sum_ref[...] = jnp.where(row == 0, jnp.broadcast_to(total, (8, tokens)), second_sum_ref[...])
        keep_ref[...] = out_ref[me]
        send_ref[...] = out_ref[1 - me]

    outs = [jax.ShapeDtypeStruct((tokens, share), BF16)] * 2
    outs += [jax.ShapeDtypeStruct((8, tokens), F32)]
    scratch = [VMEM((share, tokens), BF16), VMEM((TEAM, tokens, share), BF16)]
    args = [rim_q, raw, ear, part, keys, values, second, second_sum, starts]
    return kernel_call(body, outs, args, scratch, 2 * share * tokens * 2 * tokens * 8)


def scaled(parts, sums, gain, total_channels, count_got):
    tokens, share = parts[0].shape
    count = len(sums)

    pieces = 4
    rows = tokens // pieces

    def body(*refs):
        part_refs, sum_refs = refs[:TEAM], refs[TEAM : TEAM + count]
        gain_ref, out_ref, held, sems = refs[TEAM + count :]
        me = place()
        total = jnp.zeros((1, tokens), F32)
        for ref in sum_refs:
            total = total + ref[pl.ds(me, 1), :]
        total = jnp.broadcast_to(total, (128, tokens)).T
        gains = [
            gain_ref[:, pl.ds(pl.multiple_of(lax.bitwise_xor(me, step) * share, share), share)]
            for step in range(TEAM)
        ]
        copies = []
        for piece in range(pieces):
            at = slice(piece * rows, (piece + 1) * rows)
            wides = [ref[at].astype(F32) for ref in part_refs]
            sums = total[at]
            if count_got:
                sums = sums + jnp.sum(wides[1] * wides[1], axis=1, keepdims=True)
            scale = lax.rsqrt(sums / total_channels + 1e-06)
            scale = jnp.concatenate([scale] * (share // 128), 1)
            for step in range(TEAM):
                first = pl.multiple_of(lax.bitwise_xor(me, step) * share, share)
                done = (wides[step] * scale * gains[step].astype(F32)).astype(BF16)
                held[at, pl.ds(first, share)] = done
            copy = pltpu.make_async_copy(held.at[at], out_ref.at[at], sems.at[piece])
            copy.start()
            copies.append(copy)
        for copy in copies:
            copy.wait()

    out = jax.ShapeDtypeStruct((tokens, TEAM * share), BF16)
    args = list(parts) + list(sums) + [gain.reshape(1, TEAM * share)]
    scratch = [VMEM((tokens, TEAM * share), BF16), pltpu.SemaphoreType.DMA((pieces,))]
    return kernel_call(body, [out], args, scratch, out_spaces=[pltpu.HBM])[0]


def swapped(value):
    count = lax.axis_size("seq")
    return lax.ppermute(value, "seq", [(i, i ^ 1) for i in range(count)])


def onward(value):
    count = lax.axis_size("seq")
    return lax.ppermute(value, "seq", [(i, i + TEAM) for i in range(count - TEAM)])


def per_device(q_in, k_in, v_in, filters, lengths, gain):
    tokens, channels = q_in.shape
    kv_own, k_other, v_other, starts = cut_keys_values(k_in, v_in, lengths)
    k_got = swapped(k_other)
    v_got = swapped(v_other)
    q_own, q_other = cut_queries(q_in)
    q_other, k_got = lax.optimization_barrier((q_other, k_got))
    q_got = swapped(q_other)
    rim_own = onward(kv_own)
    kv_got = jnp.stack([k_got, v_got])
    rim_got = onward(kv_got)
    rim_q = onward(second_queries(q_own, q_got, kv_got))
    raw, ear, part, q1, k1, v1 = second_conv(q_own, q_got, kv_own, kv_got, filters)
    keys, values, second, second_sum = rim_keys(rim_own, rim_got, raw, q1, k1, v1, filters, starts)
    keep, send, own = first_attention(
        rim_q, raw, ear, part, keys, values, second, second_sum, starts
    )
    mine = [keep, swapped(send)]
    head_count = lax.axis_size("head")
    if head_count == 2:
        cross = [(i, i ^ 3) for i in range(2 * lax.axis_size("seq"))]
        sums = [
            own,
            lax.ppermute(own, "head", [(0, 1), (1, 0)]),
            lax.ppermute(own, ("seq", "head"), cross),
        ]
        return scaled(mine, sums, gain, channels * head_count, True)
    own = lax.psum(own, "head")
    return scaled(mine, [own, swapped(own)], gain, channels * head_count, False)


def solution(mesh):
    placed = (
        P("seq", "head"),
        P("seq", "head"),
        P("seq", "head"),
        P(None, "head", None),
        P(),
        P("head"),
    )
    return jax.shard_map(
        per_device, mesh=mesh, in_specs=placed, out_specs=P("seq", "head"), check_vma=False
    )
```

time: 29.7 us -> 29.4 us (0.990)
    ppermute x3, waiting for transfers between devices: 2.78 us -> 2.42 us  [onward(): lax.ppermute(value, 'seq', [(i, i + TEAM) for i in range(count - TEAM)])]
  transfers between devices with their start and end apart: 9 -> 9, of which waited for: 5 -> 5; matrix products, arithmetic and copies ran while one was open for 0% -> 0% of each run, Pallas kernels for 9% -> 10%
where the time goes in v4:
time: 29.4 us; the launch traced here: 29.2 us
  starting transfers between devices  16.8 us (57%)
  waiting for transfers between devices  6.53 us (22%)
  Pallas kernels  5.71 us (19%)
    ppermute x3, starting transfers between devices, onward(): lax.ppermute(value, 'seq', [(i, i + TEAM) for i in range(count - TEAM)])  9.43 us
    pallas_call x7, Pallas kernels, kernel_call(): pl.pallas_call(body, out_shape=outs, in_specs=[pl.BlockSpec(memory_space=...  5.71 us
    ppermute x4, starting transfers between devices, swapped(): return lax.ppermute(value, 'seq', [(i, i ^ 1) for i in range(count)])  4.09 us
    ppermute x1, starting transfers between devices, per_device(): lax.ppermute(own, 'head', [(0, 1), (1, 0)])  3.15 us
    ppermute x3, waiting for transfers between devices, onward(): lax.ppermute(value, 'seq', [(i, i + TEAM) for i in range(count - TEAM)])  2.42 us
    ppermute x1, waiting for transfers between devices, per_device(): lax.ppermute(own, ('seq', 'head'), cross)  2.3 us
    ppermute x4, waiting for transfers between devices, swapped(): return lax.ppermute(value, 'seq', [(i, i ^ 1) for i in range(count)])  1.13 us
    ppermute x1, waiting for transfers between devices, per_device(): lax.ppermute(own, 'head', [(0, 1), (1, 0)])  0.67 us
  transfers between devices with their start and end apart: 9, of which 5 were waited for; matrix products, arithmetic and copies ran while one was open for 0% of the time, Pallas kernels for 10%

profile of v4, /device:TPU:9, one launch (start us, length us, event | category | flops | bytes accessed | tf_op | source)
XLA Modules:
  0.0 29.2 jit_solution(6452323713643947110)
XLA Ops:
  0.0 1.2 %shard_map.65 = (bf16[2,128,512]{2,1,0:T(8,128)(2,1)S(1)}, bf16[128,512]{1,0:T(8,128)(2,1)S(1)}, bf16[128,512]{1,0:T(8,128)(2,1)S(1)}, s32[2,128]{1,0:T(2,128)S(1)}) custom-call(bf16[128,1024]{1,0:T(8,128)(2,1)} %k_ref.1, bf16[128,1024]{1,0:T(8,128)(2,1)} %v_ref.1, s32[1,32]{1,0:T(1,128)} %bitcast.5), custom_call_target="tpu_custom_call" | custom-call | bytes 1049728 | tf_op jit(solution)/shard_map/pallas_call | solution.py:21
  1.2 1.3 %collective-permute-start = (bf16[128,512]{1,0:T(8,128)(2,1)S(1)}, bf16[128,512]{1,0:T(8,128)(2,1)S(1)}, u32[]{:S(2)}, u32[]{:S(2)}) collective-permute-start(bf16[128,512]{1,0:T(8,128)(2,1)S(1)} %get-tuple-element.28), channel_id=1, source_target_pairs={{0,2},{2,0},{4,6},{6,4},{8,10},{10,8},{12,14},{14,12},{16,18},{18,... | collective-permute-start | bytes 393224 | tf_op jit(solution)/shard_map/ppermute | solution.py:356
  2.5 0.3 collective-permute-start.2
  2.7 3.1 %collective-permute-start.4 = (bf16[2,128,512]{2,1,0:T(8,128)(2,1)S(1)}, bf16[2,128,512]{2,1,0:T(8,128)(2,1)S(1)}, u32[]{:S(2)}, u32[]{:S(2)}) collective-permute-start(bf16[2,128,512]{2,1,0:T(8,128)(2,1)S(1)} %get-tuple-element.32.kv_own_ref), channel_id=1, source_target_pairs={{0,4},{2,6},{4,8},{6,10},{8,12},{10,14},{12,16},{14,18},{16,20},{1... | collective-permute-start | bytes 786440 | tf_op jit(solution)/shard_map/ppermute | solution.py:361
  5.9 0.1 shard_map.64
  6.0 1.3 %collective-permute-start.1 = (bf16[512,128]{1,0:T(8,128)(2,1)S(1)}, bf16[512,128]{1,0:T(8,128)(2,1)S(1)}, u32[]{:S(2)}, u32[]{:S(2)}) collective-permute-start(bf16[512,128]{1,0:T(8,128)(2,1)S(1)} %get-tuple-element.29), channel_id=1, source_target_pairs={{0,2},{2,0},{4,6},{6,4},{8,10},{10,8},{12,14},{14,12},{16,18},{18,... | collective-permute-start | bytes 393224 | tf_op jit(solution)/shard_map/ppermute | solution.py:356
  7.3 1.1 %collective-permute-done.2 = bf16[128,512]{1,0:T(8,128)(2,1)S(1)} collective-permute-done((bf16[128,512]{1,0:T(8,128)(2,1)S(1)}, bf16[128,512]{1,0:T(8,128)(2,1)S(1)}, u32[]{:S(2)}, u32[]{:S(2)}) %collective-permute-start.2) | collective-permute-done | bytes 131104 | tf_op jit(solution)/shard_map/ppermute | solution.py:356
  8.5 3.1 %collective-permute-start.5 = (bf16[2,128,512]{2,1,0:T(8,128)(2,1)S(1)}, bf16[2,128,512]{2,1,0:T(8,128)(2,1)S(1)}, u32[]{:S(2)}, u32[]{:S(2)}) collective-permute-start(bf16[2,128,512]{2,1,0:T(8,128)(2,1)S(1)} %pad_maximum_fusion.after_ref.kv_got_ref), channel_id=1, source_target_pairs={{0,4},{2,6},{4,8},{6,10},{8,12},{10,14},{12,16},{14,18},{16,20},{1... | collective-permute-start | bytes 786440 | tf_op jit(solution)/shard_map/ppermute | solution.py:361
  11.6 0.0 collective-permute-done.1.got_ref.q_got_ref
  11.6 0.0 copy-start.1
  11.7 3.1 %collective-permute-start.3 = (bf16[512,128]{1,0:T(8,128)(2,1)S(1)}, bf16[512,128]{1,0:T(8,128)(2,1)S(1)}, u32[]{:S(2)}, u32[]{:S(2)}) collective-permute-start(bf16[512,128]{1,0:T(8,128)(2,1)S(1)} %shard_map.66), channel_id=1, source_target_pairs={{0,4},{2,6},{4,8},{6,10},{8,12},{10,14},{12,16},{14,18},{16,20},{1... | collective-permute-start | bytes 393224 | tf_op jit(solution)/shard_map/ppermute | solution.py:361
  14.9 1.3 %shard_map.67 = (bf16[3,512,128]{2,1,0:T(8,128)(2,1)S(1)}, bf16[4096,128]{1,0:T(8,128)(2,1)S(1)}, f32[512,128]{1,0:T(8,128)S(1)}, bf16[512,128]{1,0:T(8,128)(2,1...) custom-call(bf16[512,128]{1,0:T(8,128)(2,1)S(1)} %get-tuple-element.26.own_ref.q_own_ref, ...), custom_call_target="tpu_custom_call" | custom-call | flops 805306368 | bytes 2932736 | tf_op jit(solution)/shard_map/pallas_call | solution.py:21
  16.2 0.0 collective-permute-done.4.own_ref
  16.2 0.6 %collective-permute-done.5.got_ref = bf16[2,128,512]{2,1,0:T(8,128)(2,1)S(1)} collective-permute-done((bf16[2,128,512]{2,1,0:T(8,128)(2,1)S(1)}, bf16[2,128,512]{2,1,0:T(8,128)(2,1)S(1)}, u32[]{:S(2)}, u32[]{:S(2)}) %collective-permute-start.5) | collective-permute-done | bytes 262176 | tf_op jit(solution)/shard_map/ppermute | solution.py:361
  16.8 1.3 %shard_map.68 = (bf16[256,512]{1,0:T(8,128)(2,1)S(1)}, bf16[512,256]{1,0:T(8,128)(2,1)S(1)}, bf16[128,512]{1,0:T(8,128)(2,1)S(1)}, f32[8,128]{1,0:T(8,128)S(1)}) custom-call(bf16[2,128,512]{2,1,0:T(8,128)(2,1)S(1)} %collective-permute-done.4.own_ref, bf16[2,128,512]{2,1,0:T(8,128)(2,1)S(1)} %collective-permute-done.5.got_ref, ...), custom_call_target="tpu_custom_call" | custom-call | flops 536870912 | bytes 2020352 | tf_op jit(solution)/shard_map/pallas_call | solution.py:21
  18.1 1.8 %collective-permute-done.3.rim_ref = bf16[512,128]{1,0:T(8,128)(2,1)S(1)} collective-permute-done((bf16[512,128]{1,0:T(8,128)(2,1)S(1)}, bf16[512,128]{1,0:T(8,128)(2,1)S(1)}, u32[]{:S(2)}, u32[]{:S(2)}) %collective-permute-start.3) | collective-permute-done | bytes 131104 | tf_op jit(solution)/shard_map/ppermute | solution.py:361
  19.9 0.9 %shard_map.69 = (bf16[128,512]{1,0:T(8,128)(2,1)S(1)}, bf16[128,512]{1,0:T(8,128)(2,1)S(1)}, f32[8,128]{1,0:T(8,128)S(1)}) custom-call(bf16[512,128]{1,0:T(8,128)(2,1)S(1)} %collective-permute-done.3.rim_ref, bf16[3,512,128]{2,1,0:T(8,128)(2,1)S(1)} %get-tuple-element.33.raw_ref, bf16[4096,128]{1,0:T(8,128)(2,1)S(1)} %get-tuple-element.34.ear_ref, ...), custom_call_target="tpu_custom_call" | custom-call | flops 268435456 | bytes 2761728 | tf_op jit(solution)/shard_map/pallas_call | solution.py:21
  20.8 0.0 copy-start.2
  20.8 1.3 %collective-permute-start.6 = (bf16[128,512]{1,0:T(8,128)(2,1)S(1)}, bf16[128,512]{1,0:T(8,128)(2,1)S(1)}, u32[]{:S(2)}, u32[]{:S(2)}) collective-permute-start(bf16[128,512]{1,0:T(8,128)(2,1)S(1)} %get-tuple-element.45), channel_id=1, source_target_pairs={{0,2},{2,0},{4,6},{6,4},{8,10},{10,8},{12,14},{14,12},{16,18},{18,... | collective-permute-start | bytes 393224 | tf_op jit(solution)/shard_map/ppermute | solution.py:356
  22.1 3.2 %collective-permute-start.7 = (f32[8,128]{1,0:T(8,128)S(1)}, f32[8,128]{1,0:T(8,128)S(1)}, u32[]{:S(2)}, u32[]{:S(2)}) collective-permute-start(f32[8,128]{1,0:T(8,128)S(1)} %get-tuple-element.46.refs_2_), channel_id=1, source_target_pairs={{0,1},{1,0},{2,3},{3,2},{4,5},{5,4},{6,7},{7,6},{8,9},{9,8},{10,11... | collective-permute-start | bytes 12296 | tf_op jit(solution)/shard_map/ppermute | solution.py:387
  25.2 0.1 collective-permute-start.8
  25.4 0.7 %collective-permute-done.7.refs_3_ = f32[8,128]{1,0:T(8,128)S(1)} collective-permute-done((f32[8,128]{1,0:T(8,128)S(1)}, f32[8,128]{1,0:T(8,128)S(1)}, u32[]{:S(2)}, u32[]{:S(2)}) %collective-permute-start.7) | collective-permute-done | bytes 4128 | tf_op jit(solution)/shard_map/ppermute | solution.py:387
  26.0 2.3 %collective-permute-done.8.refs_4_ = f32[8,128]{1,0:T(8,128)S(1)} collective-permute-done((f32[8,128]{1,0:T(8,128)S(1)}, f32[8,128]{1,0:T(8,128)S(1)}, u32[]{:S(2)}, u32[]{:S(2)}) %collective-permute-start.8) | collective-permute-done | bytes 4128 | tf_op jit(solution)/shard_map/ppermute | solution.py:388
  28.3 0.9 %shard_map.70 = bf16[128,1024]{1,0:T(8,128)(2,1)} custom-call(bf16[128,512]{1,0:T(8,128)(2,1)S(1)} %get-tuple-element.44.refs_0_, bf16[128,512]{1,0:T(8,128)(2,1)S(1)} %collective-permute-done.6.refs_1_, f32[8,128]{1,0:T(8,128)S(1)} %get-tuple-element.46.refs_2_, f32[8,128]{1,0:T(8,128)S(1)} %collective-permute-done.7.refs_3_, ...), custom_call_target="tpu_custom_call" | custom-call | bytes 538624 | tf_op jit(solution)/shard_map/pallas_call | solution.py:21
  (9 shorter events, 0.1 us)
Async XLA Ops:
  0.0 5.9 %copy-start = (bf16[128,1024]{1,0:T(8,128)(2,1)S(1)}, bf16[128,1024]{1,0:T(8,128)(2,1)}, u32[]{:S(2)}) copy-start(bf16[128,1024]{1,0:T(8,128)(2,1)} %ref.1) | copy-start | bytes 786436
  1.2 4.8 %collective-permute-start = (bf16[128,512]{1,0:T(8,128)(2,1)S(1)}, bf16[128,512]{1,0:T(8,128)(2,1)S(1)}, u32[]{:S(2)}, u32[]{:S(2)}) collective-permute-start(bf16[128,512]{1,0:T(8,128)(2,1)S(1)} %get-tuple-element.28), channel_id=1, source_target_pairs={{0,2},{2,0},{4,6},{6,4},{8,10},{10,8},{12,14},{14,12},{16,18},{18,... | collective-permute-start | bytes 393224 | tf_op jit(solution)/shard_map/ppermute | solution.py:356
  2.5 6.0 %collective-permute-start.2 = (bf16[128,512]{1,0:T(8,128)(2,1)S(1)}, bf16[128,512]{1,0:T(8,128)(2,1)S(1)}, u32[]{:S(2)}, u32[]{:S(2)}) collective-permute-start(bf16[128,512]{1,0:T(8,128)(2,1)S(1)} %get-tuple-element.31), channel_id=1, source_target_pairs={{0,2},{2,0},{4,6},{6,4},{8,10},{10,8},{12,14},{14,12},{16,18},{18,... | collective-permute-start | bytes 393224 | tf_op jit(solution)/shard_map/ppermute | solution.py:356
  2.7 13.4 %collective-permute-start.4 = (bf16[2,128,512]{2,1,0:T(8,128)(2,1)S(1)}, bf16[2,128,512]{2,1,0:T(8,128)(2,1)S(1)}, u32[]{:S(2)}, u32[]{:S(2)}) collective-permute-start(bf16[2,128,512]{2,1,0:T(8,128)(2,1)S(1)} %get-tuple-element.32.kv_own_ref), channel_id=1, source_target_pairs={{0,4},{2,6},{4,8},{6,10},{8,12},{10,14},{12,16},{14,18},{16,20},{1... | collective-permute-start | bytes 786440 | tf_op jit(solution)/shard_map/ppermute | solution.py:361
  6.0 5.6 %collective-permute-start.1 = (bf16[512,128]{1,0:T(8,128)(2,1)S(1)}, bf16[512,128]{1,0:T(8,128)(2,1)S(1)}, u32[]{:S(2)}, u32[]{:S(2)}) collective-permute-start(bf16[512,128]{1,0:T(8,128)(2,1)S(1)} %get-tuple-element.29), channel_id=1, source_target_pairs={{0,2},{2,0},{4,6},{6,4},{8,10},{10,8},{12,14},{14,12},{16,18},{18,... | collective-permute-start | bytes 393224 | tf_op jit(solution)/shard_map/ppermute | solution.py:356
  8.5 8.3 %collective-permute-start.5 = (bf16[2,128,512]{2,1,0:T(8,128)(2,1)S(1)}, bf16[2,128,512]{2,1,0:T(8,128)(2,1)S(1)}, u32[]{:S(2)}, u32[]{:S(2)}) collective-permute-start(bf16[2,128,512]{2,1,0:T(8,128)(2,1)S(1)} %pad_maximum_fusion.after_ref.kv_got_ref), channel_id=1, source_target_pairs={{0,4},{2,6},{4,8},{6,10},{8,12},{10,14},{12,16},{14,18},{16,20},{1... | collective-permute-start | bytes 786440 | tf_op jit(solution)/shard_map/ppermute | solution.py:361
  11.6 3.2 %copy-start.1 = (bf16[3,64,128]{2,1,0:T(8,128)(2,1)S(1)}, bf16[3,64,128]{2,1,0:T(8,128)(2,1)}, u32[]{:S(2)}) copy-start(bf16[3,64,128]{2,1,0:T(8,128)(2,1)} %filter_ref.3) | copy-start | bytes 147460
  11.7 8.2 %collective-permute-start.3 = (bf16[512,128]{1,0:T(8,128)(2,1)S(1)}, bf16[512,128]{1,0:T(8,128)(2,1)S(1)}, u32[]{:S(2)}, u32[]{:S(2)}) collective-permute-start(bf16[512,128]{1,0:T(8,128)(2,1)S(1)} %shard_map.66), channel_id=1, source_target_pairs={{0,4},{2,6},{4,8},{6,10},{8,12},{10,14},{12,16},{14,18},{16,20},{1... | collective-permute-start | bytes 393224 | tf_op jit(solution)/shard_map/ppermute | solution.py:361
  20.8 4.6 %copy-start.2 = (bf16[1024]{0:T(1024)(128)(2,1)S(1)}, bf16[1024]{0:T(1024)(128)(2,1)}, u32[]{:S(2)}) copy-start(bf16[1024]{0:T(1024)(128)(2,1)} %param.11) | copy-start | bytes 6148
  20.8 7.6 %collective-permute-start.6 = (bf16[128,512]{1,0:T(8,128)(2,1)S(1)}, bf16[128,512]{1,0:T(8,128)(2,1)S(1)}, u32[]{:S(2)}, u32[]{:S(2)}) collective-permute-start(bf16[128,512]{1,0:T(8,128)(2,1)S(1)} %get-tuple-element.45), channel_id=1, source_target_pairs={{0,2},{2,0},{4,6},{6,4},{8,10},{10,8},{12,14},{14,12},{16,18},{18,... | collective-permute-start | bytes 393224 | tf_op jit(solution)/shard_map/ppermute | solution.py:356
  22.1 4.0 %collective-permute-start.7 = (f32[8,128]{1,0:T(8,128)S(1)}, f32[8,128]{1,0:T(8,128)S(1)}, u32[]{:S(2)}, u32[]{:S(2)}) collective-permute-start(f32[8,128]{1,0:T(8,128)S(1)} %get-tuple-element.46.refs_2_), channel_id=1, source_target_pairs={{0,1},{1,0},{2,3},{3,2},{4,5},{5,4},{6,7},{7,6},{8,9},{9,8},{10,11... | collective-permute-start | bytes 12296 | tf_op jit(solution)/shard_map/ppermute | solution.py:387
  25.2 3.1 %collective-permute-start.8 = (f32[8,128]{1,0:T(8,128)S(1)}, f32[8,128]{1,0:T(8,128)S(1)}, u32[]{:S(2)}, u32[]{:S(2)}) collective-permute-start(f32[8,128]{1,0:T(8,128)S(1)} %get-tuple-element.46.refs_2_), channel_id=1, source_target_pairs={{0,3},{1,2},{2,1},{3,0},{4,7},{5,6},{6,5},{7,4},{8,11},{9,10},{10,... | collective-permute-start | bytes 12296 | tf_op jit(solution)/shard_map/ppermute | solution.py:388
